TPU v7x, 256 devices: a whole 4x4x8 slice. The times are simulated.
256 devices in a mesh: pb: 32 (over z_lo, x, core), kv: 8 (over z_hi, y).
Axes of the slice: x: 4, y: 4, z: 8 (z_hi: 2, z_lo: 4; z = z_hi * 4 + z_lo), core: 2. Of those that a mesh axis runs over, the one named last changes fastest.
Arguments:
- queries: bfloat16 [32768, 2048], P(('pb', 'kv')), may hold values from -120.20815 to 120.20815
- key_vectors: bfloat16 [32768, 512], P(('pb', 'kv')), may hold values from -4 to 4
- value_vectors: bfloat16 [32768, 512], P(('pb', 'kv')), may hold values from -6 to 6
- output_gradient: bfloat16 [32768, 2048], P(('pb', 'kv')), may hold values from -6 to 6
- doc_lengths: int32 [48], replicated, may hold values from 1 to 1024, 32768 in all
Outputs:
- query_grad: bfloat16 [32768, 2048], P(('pb', 'kv'))
- key_gradient: bfloat16 [32768, 512], P(('pb', 'kv'))
- value_gradient: bfloat16 [32768, 512], P(('pb', 'kv'))
Inputs may be any that keep to these rules, and one draw needn't show every extreme that they name: `doc_lengths`: the 48 lengths sum to 32768; the longest is exactly 1024.
All inputs are finite; a program needn't handle non-finite values.
Results may differ from a plain program's by a relative error of at most 0.033.
Values may be sent and summed in bfloat16 or wider, within the bound.
A program may use at most 128 MiB of HBM per device.

v0:
```python
import jax
import jax.numpy as jnp
from jax import lax
from jax.sharding import PartitionSpec as P

KEY_VALUE_HEADS = 4
HEAD_WIDTH = 128
QUERIES_PER_KEY = 4
LOOK = 1


NEG_FILL = -1e30


def shifted(x, axis, by):
    size = lax.axis_size(axis)
    pairs = [(i, i + by) for i in range(size) if 0 <= i + by < size]
    return lax.ppermute(x, axis, pairs)


def doc_index(positions, doc_ends):
    return jnp.sum((positions[:, None] >= doc_ends[None, :]).astype(jnp.int32), axis=1)


def contract_last(left, right):
    return lax.dot_general(
        left, right, (((1,), (1,)), ((), ())), preferred_element_type=jnp.float32
    )


def contract_first(left, right):
    return lax.dot_general(
        left, right, (((0,), (0,)), ((), ())), preferred_element_type=jnp.float32
    )


def local(queries, key_vectors, value_vectors, output_gradient, doc_lengths):
    count_of_rows = queries.shape[0]
    kv_count = lax.axis_size("kv")
    group_rows = kv_count * count_of_rows
    window_count = LOOK + 1
    rows_per_tile = QUERIES_PER_KEY * count_of_rows
    logit_scale = HEAD_WIDTH ** (-0.5)
    pb_index = lax.axis_index("pb")
    kv_index = lax.axis_index("kv")
    doc_ends = jnp.cumsum(doc_lengths)
    group_keys, group_values = (
        lax.all_gather(key_vectors, "kv", axis=0, tiled=True),
        lax.all_gather(value_vectors, "kv", axis=0, tiled=True),
    )
    reached = [(group_keys, group_values)]
    stride = 1
    reached.append(shifted((group_keys, group_values), "pb", stride))
    window_key = jnp.concatenate(
        [reached[LOOK - offset][0] for offset in range(window_count)], axis=0
    )
    window_value = jnp.concatenate(
        [reached[LOOK - offset][1] for offset in range(window_count)], axis=0
    )
    query_positions = (pb_index * kv_count + kv_index) * count_of_rows + jnp.arange(
        count_of_rows, dtype=jnp.int32
    )
    query_docs = doc_index(query_positions, doc_ends)
    allowed_tiles = []
    active_tiles = []
    for segment in range(window_count):
        key_positions = (pb_index - LOOK + segment) * group_rows + jnp.arange(
            group_rows, dtype=jnp.int32
        )
        key_docs = doc_index(key_positions, doc_ends)
        allowed = (
            (key_positions[None, :] <= query_positions[:, None])
            & (key_docs[None, :] == query_docs[:, None])
            & (key_positions[None, :] >= 0)
        )
        allowed_tiles.append(jnp.tile(allowed, (QUERIES_PER_KEY, 1)))
        active_tiles.append(jnp.any(allowed))
    query_heads = (
        queries.reshape(count_of_rows, KEY_VALUE_HEADS, QUERIES_PER_KEY, HEAD_WIDTH)
        .transpose(1, 2, 0, 3)
        .reshape(KEY_VALUE_HEADS, rows_per_tile, HEAD_WIDTH)
    )
    grad_heads = (
        output_gradient.reshape(count_of_rows, KEY_VALUE_HEADS, QUERIES_PER_KEY, HEAD_WIDTH)
        .transpose(1, 2, 0, 3)
        .reshape(KEY_VALUE_HEADS, rows_per_tile, HEAD_WIDTH)
    )
    query_parts = []
    key_parts = [[] for segment in range(window_count)]
    value_parts = [[] for segment in range(window_count)]
    for group_of_heads in range(KEY_VALUE_HEADS):
        query_tile = query_heads[group_of_heads]
        grad_tile = grad_heads[group_of_heads]
        key_column = window_key[:, group_of_heads * HEAD_WIDTH : (group_of_heads + 1) * HEAD_WIDTH]
        value_column = window_value[
            :, group_of_heads * HEAD_WIDTH : (group_of_heads + 1) * HEAD_WIDTH
        ]
        logit_tiles = []
        for segment in range(window_count):

            def masked_scores(segment=segment, query_tile=query_tile, key_column=key_column):
                key_piece = key_column[segment * group_rows : (segment + 1) * group_rows]
                return jnp.where(
                    allowed_tiles[segment],
                    contract_last(query_tile, key_piece) * logit_scale,
                    NEG_FILL,
                )

            logit_tiles.append(masked_scores())
        running_max = jnp.max(logit_tiles[0], axis=1)
        segment = 1
        running_max = jnp.maximum(running_max, jnp.max(logit_tiles[segment], axis=1))
        running_sum = jnp.zeros((rows_per_tile,), jnp.float32)
        for segment in range(window_count):
            running_sum = running_sum + jnp.sum(
                jnp.where(
                    allowed_tiles[segment],
                    jnp.exp(logit_tiles[segment] - running_max[:, None]),
                    0.0,
                ),
                axis=1,
            )
        log_total = running_max + jnp.log(running_sum)
        prob_tiles = [
            jnp.exp(
                jnp.where(
                    allowed_tiles[segment], logit_tiles[segment] - log_total[:, None], NEG_FILL
                )
            )
            for segment in range(window_count)
        ]
        low_tiles = [tile.astype(jnp.bfloat16) for tile in prob_tiles]
        attended = jnp.zeros((rows_per_tile, HEAD_WIDTH), jnp.float32)
        for segment in range(window_count):

            def weigh_values(
                segment=segment, attended=attended, value_column=value_column, low_tiles=low_tiles
            ):
                value_piece = value_column[segment * group_rows : (segment + 1) * group_rows]
                return attended + jnp.dot(
                    low_tiles[segment], value_piece, preferred_element_type=jnp.float32
                )

            attended = weigh_values()
        row_delta = jnp.sum(grad_tile.astype(jnp.float32) * attended, axis=1)
        query_total = jnp.zeros((rows_per_tile, HEAD_WIDTH), jnp.float32)
        for segment in range(window_count):

            def backward(
                segment=segment,
                query_total=query_total,
                prob_tiles=prob_tiles,
                low_tiles=low_tiles,
                row_delta=row_delta,
                query_tile=query_tile,
                grad_tile=grad_tile,
                key_column=key_column,
                value_column=value_column,
            ):
                key_piece = key_column[segment * group_rows : (segment + 1) * group_rows]
                value_piece = value_column[segment * group_rows : (segment + 1) * group_rows]
                prob_grad = contract_last(grad_tile, value_piece)
                score_grad = (prob_tiles[segment] * (prob_grad - row_delta[:, None])).astype(
                    jnp.bfloat16
                )
                return (
                    query_total
                    + jnp.dot(score_grad, key_piece, preferred_element_type=jnp.float32),
                    contract_first(score_grad, query_tile),
                    contract_first(low_tiles[segment], grad_tile),
                )

            query_total, key_part, value_part = backward()
            key_parts[segment].append(key_part)
            value_parts[segment].append(value_part)
        query_parts.append(query_total * logit_scale)
    query_grad = (
        jnp.stack(query_parts)
        .reshape(KEY_VALUE_HEADS, QUERIES_PER_KEY, count_of_rows, HEAD_WIDTH)
        .transpose(2, 0, 1, 3)
        .reshape(count_of_rows, KEY_VALUE_HEADS * QUERIES_PER_KEY * HEAD_WIDTH)
        .astype(jnp.bfloat16)
    )
    key_window = jnp.stack(
        [jnp.concatenate(key_parts[segment], axis=1) for segment in range(window_count)]
    )
    value_window = jnp.stack(
        [jnp.concatenate(value_parts[segment], axis=1) for segment in range(window_count)]
    )
    summed_key_grad = key_window[LOOK]
    summed_value_grad = value_window[LOOK]
    stride = 1
    back_keys = shifted(key_window[LOOK - stride].astype(jnp.bfloat16), "pb", -stride).astype(
        jnp.float32
    )
    back_values = shifted(value_window[LOOK - stride].astype(jnp.bfloat16), "pb", -stride).astype(
        jnp.float32
    )
    summed_key_grad = summed_key_grad + back_keys
    summed_value_grad = summed_value_grad + back_values
    summed_key_grad, summed_value_grad = (
        lax.psum_scatter(
            summed_key_grad.astype(jnp.bfloat16), "kv", scatter_dimension=0, tiled=True
        ).astype(jnp.float32),
        lax.psum_scatter(
            summed_value_grad.astype(jnp.bfloat16), "kv", scatter_dimension=0, tiled=True
        ).astype(jnp.float32),
    )
    key_gradient = (summed_key_grad * logit_scale).astype(jnp.bfloat16)
    value_gradient = summed_value_grad.astype(jnp.bfloat16)
    return (query_grad, key_gradient, value_gradient)


def solution(mesh):
    in_specs = (
        P(("pb", "kv"), None),
        P(("pb", "kv"), None),
        P(("pb", "kv"), None),
        P(("pb", "kv"), None),
        P(),
    )
    out_specs = (P(("pb", "kv"), None), P(("pb", "kv"), None), P(("pb", "kv"), None))
    return jax.shard_map(local, mesh=mesh, in_specs=in_specs, out_specs=out_specs, check_vma=False)
```

profile of v0, /device:TPU:7, one launch (start us, length us, event | category | flops | bytes accessed | tf_op | source)
XLA Modules:
  0.0 359.3 jit_solution(12066404508701922530)
XLA Ops:
  8.7 1.3 copy.39
  10.0 64.1 %all-gather.3.cloned.1.call-done = bf16[1024,512]{1,0:T(8,128)(2,1)} async-done(((bf16[128,512]{1,0:T(8,128)(2,1)}), bf16[1024,512]{1,0:T(8,128)(2,1)}) %all-gather.3.cloned.1.call-update) | async-done | bytes 1048592 | tf_op jit(solution)/shard_map/all_gather | solution.py:48
  74.1 4.2 %collective-permute-start = (bf16[1024,512]{1,0:T(8,128)(2,1)}, bf16[1024,512]{1,0:T(8,128)(2,1)S(1)}, u32[]{:S(2)}, u32[]{:S(2)}) collective-permute-start(bf16[1024,512]{1,0:T(8,128)(2,1)} %all-gather.3.cloned.1.call-done), channel_id=1, source_target_pairs={{0,8},{8,16},{16,24},{24,32},{32,40},{40,48},{48,56},{56,64},{64,7... | collective-permute-start | bytes 3145736 | tf_op jit(solution)/shard_map/ppermute | solution.py:18
  79.3 1.2 reshape.308
  80.4 1.5 copy.41
  82.6 0.9 fusion.118
  83.4 50.8 %all-gather.5.cloned.1.call-done = bf16[1024,512]{1,0:T(8,128)(2,1)} async-done(((bf16[128,512]{1,0:T(8,128)(2,1)}), bf16[1024,512]{1,0:T(8,128)(2,1)}) %all-gather.5.cloned.1.call-update) | async-done | bytes 1048592 | tf_op jit(solution)/shard_map/all_gather | solution.py:49
  134.3 4.2 %collective-permute-start.1 = (bf16[1024,512]{1,0:T(8,128)(2,1)}, bf16[1024,512]{1,0:T(8,128)(2,1)S(1)}, u32[]{:S(2)}, u32[]{:S(2)}) collective-permute-start(bf16[1024,512]{1,0:T(8,128)(2,1)} %all-gather.5.cloned.1.call-done), channel_id=1, source_target_pairs={{0,8},{8,16},{16,24},{24,32},{32,40},{40,48},{48,56},{56,64},{64,7... | collective-permute-start | bytes 3145736 | tf_op jit(solution)/shard_map/ppermute | solution.py:18
  143.3 4.1 %fusion = (f32[512]{0:T(512)S(1)}, f32[512]{0:T(512)S(1)}, f32[512]{0:T(512)S(1)}, f32[512]{0:T(512)S(1)}, f32[512]{0:T(512)S(1)}, /*index=5*/f32[512]{0:T(512)S(1)}, f32[512]{0:T(512)S(1)}, f32[512]{0:T(512)S(1)}) fusion(f32[512,1024]{1,0:T(8,128)S(1)} %get-tuple-element.55, f32[512]{0:T(512)S(1)} %max.40, pred[128,1024]{1,0:T(8,128)(4,1)S(1)} %get-tuple-element.52, ...), kind=kLoop, calls=%fused_computation.24 | loop fusion | flops 12578816 | bytes 17063936 | tf_op jit(solution)/shard_map/reduce_sum | solution.py:115
  147.5 3.0 fusion.21
  150.6 1.3 convolution_convert_fusion.3
  152.9 0.9 multiply_convert_fusion.7
  156.6 0.9 multiply_convert_fusion.3
  159.0 0.9 multiply_convert_fusion.1
  162.6 2.4 collective-permute-start.2
  167.7 1.0 convolution_convert_fusion.1
  169.8 11.0 %collective-permute-done.2 = bf16[1024,512]{0,1:T(8,128)(2,1)S(1)} collective-permute-done((bf16[1024,512]{0,1:T(8,128)(2,1)S(1)}, bf16[1024,512]{0,1:T(8,128)(2,1)S(1)}, u32[]{:S(2)}, u32[]{:S(2)}) %collective-permute-start.2) | collective-permute-done | bytes 1048608 | tf_op jit(solution)/shard_map/ppermute | solution.py:18
  180.8 1.3 fusion.16
  182.2 2.3 copy.48
  184.6 1.6 convolution_convert_fusion
  186.2 1.6 convolution_convert_fusion.2
  188.0 2.1 collective-permute-start.3
  190.4 2.1 fusion.77
  193.4 14.5 %collective-permute-done.3 = bf16[1024,512]{0,1:T(8,128)(2,1)S(1)} collective-permute-done((bf16[1024,512]{0,1:T(8,128)(2,1)S(1)}, bf16[1024,512]{0,1:T(8,128)(2,1)S(1)}, u32[]{:S(2)}, u32[]{:S(2)}) %collective-permute-start.3) | collective-permute-done | bytes 1048608 | tf_op jit(solution)/shard_map/ppermute | solution.py:18
  208.3 1.3 copy.50
  209.7 1.5 fusion.57
  211.3 1.5 fusion.47
  212.8 1.5 fusion.67
  216.9 1.2 convert_element_type.122
  218.1 47.1 %reduce-scatter.7.cloned.1.call-done = bf16[128,512]{1,0:T(8,128)(2,1)} async-done(((bf16[1024,512]{1,0:T(8,128)(2,1)}), bf16[128,512]{1,0:T(8,128)(2,1)}) %reduce-scatter.7.cloned.1.call-update) | async-done | bytes 131088
  265.2 1.0 copy.49
  267.0 85.8 %reduce-scatter.9.cloned.1.call-done = bf16[128,512]{1,0:T(8,128)(2,1)} async-done(((bf16[1024,512]{1,0:T(8,128)(2,1)}), bf16[128,512]{1,0:T(8,128)(2,1)}) %reduce-scatter.9.cloned.1.call-update) | async-done | bytes 131088
  (162 shorter events, 24.4 us)
Async XLA Ops:
  7.2 71.2 %copy-start.42 = (s32[48]{0:T(128)S(1)}, s32[48]{0:T(128)}, u32[]{:S(2)}) copy-start(s32[48]{0:T(128)} %param.9) | copy-start | bytes 580
  7.2 72.1 %copy-start.41 = (bf16[128,2048]{1,0:T(8,128)(2,1)S(1)}, bf16[128,2048]{1,0:T(8,128)(2,1)}, u32[]{:S(2)}) copy-start(bf16[128,2048]{1,0:T(8,128)(2,1)} %param.8) | copy-start | bytes 1572868
  7.2 66.9 %all-gather.3.cloned.1.call-start = ((), (), s32[]{:S(2)}) async-start(), calls=%async_computation.2 | async-start | bytes 1179648 | tf_op jit(solution)/shard_map/all_gather | solution.py:48
  7.9 126.3 %all-gather.5.cloned.1.call-start = ((), (), s32[]{:S(2)}) async-start(), calls=%async_computation.3 | async-start | bytes 1179648 | tf_op jit(solution)/shard_map/all_gather | solution.py:49
  8.7 256.5 %reduce-scatter.7.cloned.1.call-start = ((), (), s32[]{:S(2)}) async-start(), calls=%async_computation.4 | async-start | bytes 1179648
  74.1 66.8 %collective-permute-start = (bf16[1024,512]{1,0:T(8,128)(2,1)}, bf16[1024,512]{1,0:T(8,128)(2,1)S(1)}, u32[]{:S(2)}, u32[]{:S(2)}) collective-permute-start(bf16[1024,512]{1,0:T(8,128)(2,1)} %all-gather.3.cloned.1.call-done), channel_id=1, source_target_pairs={{0,8},{8,16},{16,24},{24,32},{32,40},{40,48},{48,56},{56,64},{64,7... | collective-permute-start | bytes 3145736 | tf_op jit(solution)/shard_map/ppermute | solution.py:18
  78.8 63.9 %copy-start.30 = (bf16[1,4,128,128]{3,2,1,0:T(8,128)(2,1)}, bf16[1,4,128,128]{3,2,1,0:T(8,128)(2,1)S(1)}, u32[]{:S(2)}) copy-start(bf16[1,4,128,128]{3,2,1,0:T(8,128)(2,1)S(1)} %copy.42) | copy-start | bytes 393220
  78.8 59.7 %copy-start.26 = (bf16[1024,512]{1,0:T(8,128)(2,1)S(1)}, bf16[1024,512]{1,0:T(8,128)(2,1)}, u32[]{:S(2)}) copy-start(bf16[1024,512]{1,0:T(8,128)(2,1)} %all-gather.3.cloned.1.call-done) | copy-start | bytes 3145732
  79.0 63.1 %copy-start.32 = (bf16[1,4,128,128]{3,2,1,0:T(8,128)(2,1)}, bf16[1,4,128,128]{3,2,1,0:T(8,128)(2,1)S(1)}, u32[]{:S(2)}) copy-start(bf16[1,4,128,128]{3,2,1,0:T(8,128)(2,1)S(1)} %copy.44) | copy-start | bytes 393220
  79.1 62.4 %copy-start.34 = (bf16[1,4,128,128]{3,2,1,0:T(8,128)(2,1)}, bf16[1,4,128,128]{3,2,1,0:T(8,128)(2,1)S(1)}, u32[]{:S(2)}) copy-start(bf16[1,4,128,128]{3,2,1,0:T(8,128)(2,1)S(1)} %copy.43) | copy-start | bytes 393220
  79.3 61.6 %copy-start.36 = (bf16[1,4,128,128]{3,2,1,0:T(8,128)(2,1)}, bf16[1,4,128,128]{3,2,1,0:T(8,128)(2,1)S(1)}, u32[]{:S(2)}) copy-start(bf16[1,4,128,128]{3,2,1,0:T(8,128)(2,1)S(1)} %copy.40) | copy-start | bytes 393220
  134.3 18.1 %collective-permute-start.1 = (bf16[1024,512]{1,0:T(8,128)(2,1)}, bf16[1024,512]{1,0:T(8,128)(2,1)S(1)}, u32[]{:S(2)}, u32[]{:S(2)}) collective-permute-start(bf16[1024,512]{1,0:T(8,128)(2,1)} %all-gather.5.cloned.1.call-done), channel_id=1, source_target_pairs={{0,8},{8,16},{16,24},{24,32},{32,40},{40,48},{48,56},{56,64},{64,7... | collective-permute-start | bytes 3145736 | tf_op jit(solution)/shard_map/ppermute | solution.py:18
  147.5 3.1 copy-start.24
  147.5 4.4 %copy-start.29 = (bf16[1024,512]{1,0:T(8,128)(2,1)S(1)}, bf16[1024,512]{1,0:T(8,128)(2,1)}, u32[]{:S(2)}) copy-start(bf16[1024,512]{1,0:T(8,128)(2,1)} %all-gather.5.cloned.1.call-done) | copy-start | bytes 3145732
  150.5 7.8 %copy-start.3 = (bf16[512,1024]{1,0:T(8,128)(2,1)}, bf16[512,1024]{1,0:T(8,128)(2,1)S(1)}, u32[]{:S(2)}) copy-start(bf16[512,1024]{1,0:T(8,128)(2,1)S(1)} %get-tuple-element.49) | copy-start | bytes 3145732
  150.5 10.2 %copy-start.2 = (bf16[512,1024]{1,0:T(8,128)(2,1)}, bf16[512,1024]{1,0:T(8,128)(2,1)S(1)}, u32[]{:S(2)}) copy-start(bf16[512,1024]{1,0:T(8,128)(2,1)S(1)} %get-tuple-element.48) | copy-start | bytes 3145732
  162.2 3.8 %copy-start.10 = (bf16[512,1024]{1,0:T(8,128)(2,1)}, bf16[512,1024]{1,0:T(8,128)(2,1)S(1)}, u32[]{:S(2)}) copy-start(bf16[512,1024]{1,0:T(8,128)(2,1)S(1)} %multiply_convert_fusion.5) | copy-start | bytes 3145732
  162.6 18.2 %collective-permute-start.2 = (bf16[1024,512]{0,1:T(8,128)(2,1)S(1)}, bf16[1024,512]{0,1:T(8,128)(2,1)S(1)}, u32[]{:S(2)}, u32[]{:S(2)}) collective-permute-start(bf16[1024,512]{0,1:T(8,128)(2,1)S(1)} %pad_maximum_fusion), channel_id=1, source_target_pairs={{8,0},{16,8},{24,16},{32,24},{40,32},{48,40},{56,48},{64,56},{72,6... | collective-permute-start | bytes 3145736 | tf_op jit(solution)/shard_map/ppermute | solution.py:18
  165.9 2.8 copy-start.14
  184.5 168.3 %reduce-scatter.9.cloned.1.call-start = ((), (), s32[]{:S(2)}) async-start(), calls=%async_computation.5 | async-start | bytes 1179648
  184.6 3.3 copy-start.39
  184.6 3.3 copy-start.40
  186.2 3.8 %copy-start.1 = (bf16[512,1024]{1,0:T(8,128)(2,1)S(1)}, bf16[512,1024]{1,0:T(8,128)(2,1)}, u32[]{:S(2)}) copy-start(bf16[512,1024]{1,0:T(8,128)(2,1)} %copy-done) | copy-start | bytes 3145732
  186.2 3.8 %copy-start.25 = (bf16[1,4,128,128]{2,1,3,0:T(4,128)(2,1)S(1)}, bf16[1,4,128,128]{2,1,3,0:T(4,128)(2,1)}, u32[]{:S(2)}) copy-start(bf16[1,4,128,128]{2,1,3,0:T(4,128)(2,1)} %get-tuple-element.32) | copy-start | bytes 393220
  188.0 4.5 %copy-start.23 = (bf16[1,4,128,128]{2,1,3,0:T(4,128)(2,1)S(1)}, bf16[1,4,128,128]{2,1,3,0:T(4,128)(2,1)}, u32[]{:S(2)}) copy-start(bf16[1,4,128,128]{2,1,3,0:T(4,128)(2,1)} %get-tuple-element.34) | copy-start | bytes 393220
  188.0 19.9 %collective-permute-start.3 = (bf16[1024,512]{0,1:T(8,128)(2,1)S(1)}, bf16[1024,512]{0,1:T(8,128)(2,1)S(1)}, u32[]{:S(2)}, u32[]{:S(2)}) collective-permute-start(bf16[1024,512]{0,1:T(8,128)(2,1)S(1)} %pad_maximum_fusion.1), channel_id=1, source_target_pairs={{8,0},{16,8},{24,16},{32,24},{40,32},{48,40},{56,48},{64,56},{72,6... | collective-permute-start | bytes 3145736 | tf_op jit(solution)/shard_map/ppermute | solution.py:18
  208.3 3.0 copy-start.17
  209.6 3.1 copy-start.19
  209.7 4.6 %copy-start.5 = (bf16[512,1024]{1,0:T(8,128)(2,1)S(1)}, bf16[512,1024]{1,0:T(8,128)(2,1)}, u32[]{:S(2)}) copy-start(bf16[512,1024]{1,0:T(8,128)(2,1)} %copy-done.4) | copy-start | bytes 3145732
  209.7 4.6 %copy-start.28 = (bf16[1024,512]{1,0:T(8,128)(2,1)S(1)}, bf16[1024,512]{1,0:T(8,128)(2,1)}, u32[]{:S(2)}) copy-start(bf16[1024,512]{1,0:T(8,128)(2,1)} %copy-done.27) | copy-start | bytes 3145732
  209.7 4.6 %copy-start.38 = (f32[512,128]{1,0:T(8,128)S(1)}, f32[512,128]{1,0:T(8,128)}, u32[]{:S(2)}) copy-start(f32[512,128]{1,0:T(8,128)} %fusion.77) | copy-start | bytes 786436
  211.2 3.5 copy-start.7
  (19 other events, 29.5 us)
Sparse Core Ops, SparseCore 0:
  10.6 63.3 all-gather.2
  76.7 57.5 all-gather.4
  184.6 80.4 reduce-scatter.6
  270.0 82.7 reduce-scatter.8
where the time goes:
time: 361 us; the launch traced here: 359 us
  waiting for transfers between devices  275 us (76%)
  matrix products  33.4 us (9%)
  between operations  14.8 us (4%)
  local copies, waits for them, and re-layouts  13.5 us (4%)
  starting transfers between devices  13.1 us (4%)
  other arithmetic  9.86 us (3%)
    unnamed x6, waiting for transfers between devices  134 us
    all_gather x1, waiting for transfers between devices, local(): lax.all_gather(key_vectors, 'kv', axis=0, tiled=True)  64.1 us
    all_gather x1, waiting for transfers between devices, local(): lax.all_gather(value_vectors, 'kv', axis=0, tiled=True)  50.8 us
    ppermute x4, waiting for transfers between devices, shifted(): return lax.ppermute(x, axis, pairs)  25.5 us
    ppermute x4, starting transfers between devices, shifted(): return lax.ppermute(x, axis, pairs)  12.9 us
    dot_general x16, matrix products, contract_last(): lax.dot_general(left, right, (((1,), (1,)), ((), ())), preferred_element_...  11.6 us
    dot_general x16, matrix products, contract_first(): lax.dot_general(left, right, (((0,), (0,)), ((), ())), preferred_element_...  9.53 us
    dot_general x8, matrix products, backward(): jnp.dot(score_grad, key_piece, preferred_element_type=jnp.float32)  8.34 us
  transfers between devices with their start and end apart: 8, of which 6 were waited for; matrix products, arithmetic and copies ran while one was open for 12% of the time, Pallas kernels for 0%

commit v1 on v0

v1 whole, which is shorter than its diff:
```python
import functools

import jax
import jax.numpy as jnp
from jax import lax
from jax.experimental import pallas as pl
from jax.experimental.pallas import tpu as pltpu
from jax.sharding import PartitionSpec as P

MESH = pl.DeviceIdType.MESH
HEADS = 4
SHARE = 4
WIDTH = 128
BLOCK = 128
HALF = HEADS * BLOCK
NEAR = 5 * BLOCK
PAIR = 2 * WIDTH
HALVES = 64
UNITS = 8
SCALE = WIDTH**-0.5
RATE = SCALE * 1.4426950408889634
FILL = -1e30


def contract_last(left, right):
    return lax.dot_general(left, right, (((1,), (1,)), ((), ())), preferred_element_type=jnp.float32)


def matmul(left, right):
    return jnp.dot(left, right, preferred_element_type=jnp.float32)


def heads_to_rows(x):
    return jnp.concatenate([x[:, :WIDTH], x[:, WIDTH:]], axis=0)


def fold(x, op):
    return op(x.reshape(x.shape[0] // 8, 8, x.shape[1]), axis=0)


def wait(ref, sem):
    pltpu.make_async_copy(ref, ref, sem).wait()


def kernel(
    q_ref, k_ref, v_ref, g_ref, len_ref,
    dq_ref, dk_ref, dv_ref,
    kv, own_in, far_in, old_in, kt, qg0, qg1, starts, e1, p1, e2, p2, ds2, ds1, stat, dqt, acc1, acc2, dqs0, dqs1, far_out, relay_out, relay_in, own_out, back,
    send, own_sem, far_sem, old_sem, q_sem, relay_sem, back_sem, dq_sem,
):
    pb, column = lax.axis_index("pb"), lax.axis_index("kv")
    half = 2 * pb + column // HEADS
    y = lax.rem(column, HEADS)

    def place(shift, row):
        there = lax.rem(half + shift + HALVES, HALVES)
        return (there // 2, lax.rem(there, 2) * HEADS + row)

    def row_at(step):
        return lax.rem(y + step, HEADS)

    partners = [place(0, row_at(d)) for d in (1, 2, 3)]
    partners += [place(s, row_at(d)) for s in (1, -1) for d in range(HEADS)]
    partners += [place(2, y), place(-2, y)]
    barrier = pltpu.get_barrier_semaphore()
    for device in partners:
        pl.semaphore_signal(barrier, inc=1, device_id=device, device_id_type=MESH)

    positions = (
        lax.broadcasted_iota(jnp.int32, (8, WIDTH), 0) * BLOCK
        + lax.broadcasted_iota(jnp.int32, (8, WIDTH), 1)
        + half * HALF
    )

    def count(i, carry):
        end, start = carry
        end = end + len_ref[i]
        return end, jnp.where(positions >= end, end, start)

    _, doc_start = lax.fori_loop(
        0, len_ref.shape[0], count, (jnp.int32(0), jnp.zeros((8, WIDTH), jnp.int32))
    )
    starts[...] = doc_start - half * HALF
    acc1[...] = jnp.zeros_like(acc1)
    acc2[...] = jnp.zeros_like(acc2)
    pl.semaphore_wait(barrier, len(partners))

    started = []
    qg, dqs = (qg0, qg1), (dqs0, dqs1)

    def push(src, dst, send_sem, recv_sem, device):
        copy = pltpu.make_async_remote_copy(
            src_ref=src, dst_ref=dst, send_sem=send_sem, recv_sem=recv_sem, device_id=device, device_id_type=MESH
        )
        copy.start()
        return copy

    def push_one(src, dst, recv_sem, device):
        started.append(push(src, dst, send.at[len(started)], recv_sem, device))

    for d in range(HEADS):
        h = row_at(d)
        cols = pl.ds(pl.multiple_of(h * WIDTH, WIDTH), WIDTH)
        for part, ref in enumerate((k_ref, v_ref)):
            src = ref.at[:, cols]
            slot = pl.ds(pl.multiple_of(y * BLOCK, BLOCK), BLOCK)
            far, own = far_in.at[part, slot], own_in.at[part, slot]
            push_one(src, far, far_sem, place(1, h))
            if d == 0:
                pltpu.make_async_copy(src, own, own_sem).start()
            else:
                push_one(src, own, own_sem, place(0, h))
    for pair in range(2):
        for d in range(HEADS):
            h = row_at(d)
            cols = pl.ds(pl.multiple_of(h * SHARE * WIDTH + pair * PAIR, PAIR), PAIR)
            for part, ref in enumerate((q_ref, g_ref)):
                dst = qg[pair].at[y, part]
                sem = q_sem.at[pair]
                if d == 0:
                    pltpu.make_async_copy(ref.at[:, cols], dst, sem).start()
                else:
                    push_one(ref.at[:, cols], dst, sem, place(0, h))

    wait(own_in, own_sem)
    push_one(own_in, old_in, old_sem, place(2, y))
    kv[:, HALF : 2 * HALF] = own_in[...]
    kt[:, HALF : 2 * HALF] = own_in[0].T
    wait(old_in, old_sem)
    kv[:, 0:HALF] = old_in[...]
    kt[:, 0:HALF] = old_in[0].T

    row = lax.broadcasted_iota(jnp.int32, (BLOCK, PAIR), 0)
    token = lax.rem(lax.broadcasted_iota(jnp.int32, (BLOCK, PAIR), 1), WIDTH)

    def first_of(j):
        line = starts[pl.ds(j, 1)]
        return jnp.concatenate([line, line], axis=1)

    def scores(k_of, q, j, blocks, key_base, out, causal_last):
        first = first_of(j)
        top = jnp.full((8, PAIR), FILL, jnp.float32)
        for b in range(blocks):
            s = contract_last(k_of(b), q)
            keep = row >= first - key_base(b)
            if causal_last and b == blocks - 1:
                keep = keep & (row <= token)
            s = jnp.where(keep, s, FILL)
            out[b * BLOCK : (b + 1) * BLOCK] = s
            top = jnp.maximum(top, fold(s, jnp.max))
        return jnp.max(top, axis=0, keepdims=True)

    def weights(v_of, g, blocks, top, e_out, p_out):
        shift = top * RATE
        total = jnp.zeros((8, PAIR), jnp.float32)
        delta = jnp.zeros((8, PAIR), jnp.float32)
        for b in range(blocks):
            rows = slice(b * BLOCK, (b + 1) * BLOCK)
            e = jnp.exp2(e_out[rows] * RATE - shift)
            e_out[rows] = e
            p = contract_last(v_of(b), g)
            p_out[rows] = p
            total = total + fold(e, jnp.sum)
            delta = delta + fold(e * p, jnp.sum)
        return jnp.sum(total, axis=0, keepdims=True), jnp.sum(delta, axis=0, keepdims=True)

    def near_scores(pair, j, _):
        u = pair * HEADS + j
        q = heads_to_rows(qg[pair][j, 0])
        g = heads_to_rows(qg[pair][j, 1])

        def near_rows(part):
            return lambda b: kv[part, pl.ds(pl.multiple_of((j + b) * BLOCK, BLOCK), BLOCK)]

        def key_base(b):
            block = j + b
            return jnp.where(block < HEADS, block * BLOCK - 2 * HALF, (block - HEADS) * BLOCK)

        top = scores(near_rows(0), q, j, 5, key_base, e1.at[u], True)
        total, delta = weights(near_rows(1), g, 5, top, e1.at[u], p1.at[u])
        stat[u, 0:1] = top
        stat[u, 1:2] = total
        stat[u, 2:3] = delta
        return 0

    for pair in range(2):
        wait(qg[pair], q_sem.at[pair])
        lax.fori_loop(0, HEADS, functools.partial(near_scores, pair), 0)

    wait(far_in, far_sem)
    kt[:, 2 * HALF : 3 * HALF] = far_in[0].T

    def far_work(pair, j, _):
        u = pair * HEADS + j
        q = heads_to_rows(qg[pair][j, 0])
        g = heads_to_rows(qg[pair][j, 1])

        def far_rows(part):
            return lambda b: far_in[part, b * BLOCK : (b + 1) * BLOCK]

        top2 = scores(far_rows(0), q, j, 4, lambda b: b * BLOCK - HALF, e2, False)
        total2, delta2 = weights(far_rows(1), g, 4, top2, e2, p2)
        top1, total1, delta1 = stat[u, 0:1], stat[u, 1:2], stat[u, 2:3]
        top = jnp.maximum(top1, top2)
        a1 = jnp.exp2((top1 - top) * RATE)
        a2 = jnp.exp2((top2 - top) * RATE)
        inverse = 1.0 / (a1 * total1 + a2 * total2)
        delta = (a1 * delta1 + a2 * delta2) * inverse
        a2 = a2 * inverse
        stat[u, 0:1] = a1 * inverse
        stat[u, 1:2] = delta
        for b in range(4):
            rows = slice(b * BLOCK, (b + 1) * BLOCK)
            p = e2[rows] * a2
            ds = (p * (p2[rows] - delta)).astype(jnp.bfloat16)
            ds2[rows] = ds
            acc2[0, rows] += matmul(ds, q)
            acc2[1, rows] += matmul(p.astype(jnp.bfloat16), g)
        dqt[u] = matmul(kt[:, 2 * HALF : 3 * HALF], ds2[...])
        return 0

    for pair in range(2):
        lax.fori_loop(0, HEADS, functools.partial(far_work, pair), 0)

    far_out[...] = acc2[...].astype(jnp.bfloat16)
    mine = pl.ds(pl.multiple_of(y * WIDTH, WIDTH), WIDTH)
    for d in range(HEADS):
        j = row_at(d)
        rows = pl.ds(pl.multiple_of(j * BLOCK, BLOCK), BLOCK)
        push_one(far_out.at[:, rows], back.at[1, :, :, mine], back_sem.at[1], place(-1, j))

    def near_work(pair, j, _):
        u = pair * HEADS + j
        q = heads_to_rows(qg[pair][j, 0])
        g = heads_to_rows(qg[pair][j, 1])
        a1, delta = stat[u, 0:1], stat[u, 1:2]
        for b in range(5):
            rows = slice(b * BLOCK, (b + 1) * BLOCK)
            p = e1[u, rows] * a1
            ds = (p * (p1[u, rows] - delta)).astype(jnp.bfloat16)
            ds1[rows] = ds
            where = pl.ds(pl.multiple_of((j + b) * BLOCK, BLOCK), BLOCK)
            acc1[0, where] += matmul(ds, q)
            acc1[1, where] += matmul(p.astype(jnp.bfloat16), g)
        total = dqt[u] + matmul(kt[:, pl.ds(pl.multiple_of(j * BLOCK, BLOCK), NEAR)], ds1[...])
        total = (total * SCALE).T.astype(jnp.bfloat16)
        dqs[pair][j] = jnp.concatenate([total[:BLOCK], total[BLOCK:]], axis=1)
        return 0

    for pair in range(2):
        lax.fori_loop(0, HEADS, functools.partial(near_work, pair), 0)
        dst = dq_ref.at[:, pl.ds(pl.multiple_of(y * SHARE * WIDTH + pair * PAIR, PAIR), PAIR)]
        for d in range(HEADS):
            j = row_at(d)
            if d == 0:
                pltpu.make_async_copy(dqs[pair].at[j], dst, dq_sem).start()
            else:
                push_one(dqs[pair].at[j], dst, dq_sem, place(0, j))

    relay_out[...] = acc1[:, 0:HALF].astype(jnp.bfloat16)
    push_one(relay_out, relay_in, relay_sem, place(-2, y))
    wait(relay_in, relay_sem)
    own_out[...] = (acc1[:, HALF : 2 * HALF] + relay_in[...].astype(jnp.float32)).astype(jnp.bfloat16)
    for d in range(HEADS):
        j = row_at(d)
        rows = pl.ds(pl.multiple_of(j * BLOCK, BLOCK), BLOCK)
        if d == 0:
            pltpu.make_async_copy(own_out.at[:, rows], back.at[0, :, :, mine], back_sem.at[0]).start()
        else:
            push_one(own_out.at[:, rows], back.at[0, :, :, mine], back_sem.at[0], place(0, j))
    wait(back.at[0], back_sem.at[0])
    wait(back.at[1], back_sem.at[1])
    dk_ref[...] = ((back[0, 0].astype(jnp.float32) + back[1, 0].astype(jnp.float32)) * SCALE).astype(jnp.bfloat16)
    dv_ref[...] = (back[0, 1].astype(jnp.float32) + back[1, 1].astype(jnp.float32)).astype(jnp.bfloat16)
    wait(dq_ref, dq_sem)
    for copy in started:
        copy.wait_send()


def local(queries, key_vectors, value_vectors, output_gradient, doc_lengths):
    low, full = jnp.bfloat16, jnp.float32
    wide = jax.ShapeDtypeStruct((BLOCK, HEADS * SHARE * WIDTH), low)
    narrow = jax.ShapeDtypeStruct((BLOCK, HEADS * WIDTH), low)
    anywhere = pl.BlockSpec(memory_space=pl.ANY)
    near = pl.BlockSpec(memory_space=pltpu.VMEM)
    return pl.pallas_call(
        kernel,
        out_shape=(wide, narrow, narrow),
        in_specs=[anywhere] * 4 + [pl.BlockSpec(memory_space=pltpu.SMEM)],
        out_specs=(anywhere, near, near),
        scratch_shapes=[
            pltpu.VMEM((2, 2 * HALF, WIDTH), low),
            pltpu.VMEM((2, HALF, WIDTH), low),
            pltpu.VMEM((2, HALF, WIDTH), low),
            pltpu.VMEM((2, HALF, WIDTH), low),
            pltpu.VMEM((WIDTH, 3 * HALF), low),
            pltpu.VMEM((HEADS, 2, BLOCK, PAIR), low),
            pltpu.VMEM((HEADS, 2, BLOCK, PAIR), low),
            pltpu.VMEM((8, WIDTH), jnp.int32),
            pltpu.VMEM((UNITS, NEAR, PAIR), full),
            pltpu.VMEM((UNITS, NEAR, PAIR), full),
            pltpu.VMEM((HALF, PAIR), full),
            pltpu.VMEM((HALF, PAIR), full),
            pltpu.VMEM((HALF, PAIR), low),
            pltpu.VMEM((NEAR, PAIR), low),
            pltpu.VMEM((UNITS, 8, PAIR), full),
            pltpu.VMEM((UNITS, WIDTH, PAIR), full),
            pltpu.VMEM((2, 2 * HALF, WIDTH), full),
            pltpu.VMEM((2, HALF, WIDTH), full),
            pltpu.VMEM((HEADS, BLOCK, PAIR), low),
            pltpu.VMEM((HEADS, BLOCK, PAIR), low),
            pltpu.VMEM((2, HALF, WIDTH), low),
            pltpu.VMEM((2, HALF, WIDTH), low),
            pltpu.VMEM((2, HALF, WIDTH), low),
            pltpu.VMEM((2, HALF, WIDTH), low),
            pltpu.VMEM((2, 2, BLOCK, HEADS * WIDTH), low),
            pltpu.SemaphoreType.DMA((48,)),
            pltpu.SemaphoreType.DMA,
            pltpu.SemaphoreType.DMA,
            pltpu.SemaphoreType.DMA,
            pltpu.SemaphoreType.DMA((2,)),
            pltpu.SemaphoreType.DMA,
            pltpu.SemaphoreType.DMA((2,)),
            pltpu.SemaphoreType.DMA,
        ],
        compiler_params=pltpu.CompilerParams(
            collective_id=0, has_side_effects=True, vmem_limit_bytes=40 << 20
        ),
        cost_estimate=pl.CostEstimate(flops=3 << 30, bytes_accessed=3 << 20, transcendentals=3 << 20),
    )(queries, key_vectors, value_vectors, output_gradient, doc_lengths)


def solution(mesh):
    rows = P(("pb", "kv"), None)
    return jax.shard_map(
        local, mesh=mesh, in_specs=(rows, rows, rows, rows, P()), out_specs=(rows, rows, rows), check_vma=False
    )
```

time: 361 us -> 63.6 us (0.18)
  the two profiles are of different devices: /device:TPU:7 before, /device:TPU:103 now
where the time goes in v1:
time: 63.6 us; the launch traced here: 63.3 us
  Pallas kernels  56.1 us (88%)
  local copies, waits for them, and re-layouts  6.64 us (10%)
  between operations  0.65 us (1%)
    pallas_call x1, Pallas kernels, local(): pl.pallas_call(kernel, out_shape=(wide, narrow, narrow), in_specs=[anywhe...  56.1 us
    unnamed x13, local copies, waits for them, and re-layouts  6.64 us

profile of v1, /device:TPU:103, one launch (start us, length us, event | category | flops | bytes accessed | tf_op | source)
XLA Modules:
  0.0 63.3 jit_solution(7762506832104435364)
XLA Ops:
  0.6 0.0 copy-start
  0.6 1.0 %copy-done = bf16[128,2048]{1,0:T(8,128)(2,1)S(1)} copy-done((bf16[128,2048]{1,0:T(8,128)(2,1)S(1)}, bf16[128,2048]{1,0:T(8,128)(2,1)}, u32[]{:S(2)}) %copy-start) | copy-done | bytes 524312
  1.7 0.0 copy-start.1
  1.7 1.0 %copy-done.1 = bf16[128,2048]{1,0:T(8,128)(2,1)S(1)} copy-done((bf16[128,2048]{1,0:T(8,128)(2,1)S(1)}, bf16[128,2048]{1,0:T(8,128)(2,1)}, u32[]{:S(2)}) %copy-start.1) | copy-done | bytes 524312
  2.7 0.0 copy-start.2
  2.7 0.9 %copy-done.2 = bf16[128,512]{1,0:T(8,128)(2,1)S(1)} copy-done((bf16[128,512]{1,0:T(8,128)(2,1)S(1)}, bf16[128,512]{1,0:T(8,128)(2,1)}, u32[]{:S(2)}) %copy-start.2) | copy-done | bytes 131096
  3.6 0.0 copy-start.3
  3.6 0.9 %copy-done.3 = bf16[128,512]{1,0:T(8,128)(2,1)S(1)} copy-done((bf16[128,512]{1,0:T(8,128)(2,1)S(1)}, bf16[128,512]{1,0:T(8,128)(2,1)}, u32[]{:S(2)}) %copy-start.3) | copy-done | bytes 131096
  4.5 0.0 copy-start.4
  4.5 0.7 %copy-done.4 = s32[48]{0:T(128)S(1)} copy-done((s32[48]{0:T(128)S(1)}, s32[48]{0:T(128)}, u32[]{:S(2)}) %copy-start.4) | copy-done | bytes 216
  5.2 56.1 %shard_map.76 = (bf16[128,2048]{1,0:T(8,128)(2,1)S(1)}, bf16[128,512]{1,0:T(8,128)(2,1)S(1)}, bf16[128,512]{1,0:T(8,128)(2,1)S(1)}) custom-call(bf16[128,2048]{1,0:T(8,128)(2,1)S(1)} %copy-done, bf16[128,512]{1,0:T(8,128)(2,1)S(1)} %copy-done.2, bf16[128,512]{1,0:T(8,128)(2,1)S(1)} %copy-done.3, bf16[128,2048]{1,0:T(8,128)(2,1)S(1)} %copy-done.1, ...), custom_call_target="tpu_custom_call" | custom-call | flops 3221225472 | bytes 3145728 | tf_op jit(solution)/shard_map/pallas_call | solution.py:286
  61.2 0.8 %copy.11 = bf16[128,2048]{1,0:T(8,128)(2,1)} copy(bf16[128,2048]{1,0:T(8,128)(2,1)S(1)} %get-tuple-element.6) | data formatting | bytes 1048576
  62.0 0.7 %copy.12 = bf16[128,512]{1,0:T(8,128)(2,1)} copy(bf16[128,512]{1,0:T(8,128)(2,1)S(1)} %get-tuple-element.7) | data formatting | bytes 262144
  62.7 0.7 %copy.13 = bf16[128,512]{1,0:T(8,128)(2,1)} copy(bf16[128,512]{1,0:T(8,128)(2,1)S(1)} %get-tuple-element.8) | data formatting | bytes 262144
Async XLA Ops:
  0.6 1.0 %copy-start = (bf16[128,2048]{1,0:T(8,128)(2,1)S(1)}, bf16[128,2048]{1,0:T(8,128)(2,1)}, u32[]{:S(2)}) copy-start(bf16[128,2048]{1,0:T(8,128)(2,1)} %q_ref.1) | copy-start | bytes 1572868
  1.7 1.0 %copy-start.1 = (bf16[128,2048]{1,0:T(8,128)(2,1)S(1)}, bf16[128,2048]{1,0:T(8,128)(2,1)}, u32[]{:S(2)}) copy-start(bf16[128,2048]{1,0:T(8,128)(2,1)} %g_ref.1) | copy-start | bytes 1572868
  2.7 0.9 %copy-start.2 = (bf16[128,512]{1,0:T(8,128)(2,1)S(1)}, bf16[128,512]{1,0:T(8,128)(2,1)}, u32[]{:S(2)}) copy-start(bf16[128,512]{1,0:T(8,128)(2,1)} %k_ref.1) | copy-start | bytes 393220
  3.6 0.9 %copy-start.3 = (bf16[128,512]{1,0:T(8,128)(2,1)S(1)}, bf16[128,512]{1,0:T(8,128)(2,1)}, u32[]{:S(2)}) copy-start(bf16[128,512]{1,0:T(8,128)(2,1)} %v_ref.1) | copy-start | bytes 393220
  4.5 0.7 %copy-start.4 = (s32[48]{0:T(128)S(1)}, s32[48]{0:T(128)}, u32[]{:S(2)}) copy-start(s32[48]{0:T(128)} %len_ref.1) | copy-start | bytes 580

commit v2 on v1

v2 whole, which is shorter than its diff:
```python
import functools

import jax
import jax.numpy as jnp
from jax import lax
from jax.experimental import pallas as pl
from jax.experimental.pallas import tpu as pltpu
from jax.sharding import PartitionSpec as P

MESH = pl.DeviceIdType.MESH
HEADS = 4
SHARE = 4
WIDTH = 128
BLOCK = 128
HALF = HEADS * BLOCK
NEAR = 5 * BLOCK
PAIR = 2 * WIDTH
HALVES = 64
CHUNK = 64
SCALE = WIDTH**-0.5
FILL = -1e30


def contract_last(left, right):
    return lax.dot_general(left, right, (((1,), (1,)), ((), ())), preferred_element_type=jnp.float32)


def matmul(left, right):
    return jnp.dot(left, right, preferred_element_type=jnp.float32)


def fold(x, op):
    return op(x.reshape(x.shape[0] // 8, 8, x.shape[1]), axis=0)


def wait(ref, sem):
    pltpu.make_async_copy(ref, ref, sem).wait()


def kernel(
    q_ref, k_ref, v_ref, g_ref, len_ref,
    dq_ref, dk_ref, dv_ref,
    kv, own_in, far_in, old_in, kt, kt_far, qg0, qg1, rows_of, starts,
    e1a, e1b, p1a, p1b, e2a, e2b, p2a, p2b, ds_far, pr_far, ds1a, ds1b, pr1a, pr1b,
    stat_a, stat_b, dqt_a, dqt_b, acc1, acc2, dqs0, dqs1, far_out, relay_out, relay_in, own_out, back,
    send, own_sem, far_sem, old_sem, q_sem, relay_sem, back_sem, dq_sem,
):
    qg, dqs, e1, p1, e2, p2 = (qg0, qg1), (dqs0, dqs1), (e1a, e1b), (p1a, p1b), (e2a, e2b), (p2a, p2b)
    ds1, pr1, stat, dqt = (ds1a, ds1b), (pr1a, pr1b), (stat_a, stat_b), (dqt_a, dqt_b)
    pb, column = lax.axis_index("pb"), lax.axis_index("kv")
    half = 2 * pb + column // HEADS
    y = lax.rem(column, HEADS)
    has_old = half >= 2
    has_later = half < HALVES - 2

    def place(shift, row):
        there = lax.rem(half + shift + HALVES, HALVES)
        return (there // 2, lax.rem(there, 2) * HEADS + row)

    def row_at(step):
        return lax.rem(y + step, HEADS)

    partners = [place(0, row_at(d)) for d in (1, 2, 3)]
    partners += [place(s, row_at(d)) for s in (1, -1) for d in range(HEADS)]
    barrier = pltpu.get_barrier_semaphore()
    for device in partners:
        pl.semaphore_signal(barrier, inc=1, device_id=device, device_id_type=MESH)

    @pl.when(has_later)
    def _():
        pl.semaphore_signal(barrier, inc=1, device_id=place(2, y), device_id_type=MESH)

    @pl.when(has_old)
    def _():
        pl.semaphore_signal(barrier, inc=1, device_id=place(-2, y), device_id_type=MESH)

    positions = (
        lax.broadcasted_iota(jnp.int32, (8, WIDTH), 0) * BLOCK
        + lax.broadcasted_iota(jnp.int32, (8, WIDTH), 1)
        + half * HALF
    )

    def count(i, carry):
        end, start = carry
        end = end + len_ref[i]
        return end, jnp.where(positions >= end, end, start)

    _, doc_start = lax.fori_loop(
        0, len_ref.shape[0], count, (jnp.int32(0), jnp.zeros((8, WIDTH), jnp.int32))
    )
    starts[...] = doc_start - half * HALF
    acc1[...] = jnp.zeros_like(acc1)

    @pl.when(jnp.logical_not(has_old))
    def _():
        old_in[...] = jnp.zeros_like(old_in)

    @pl.when(jnp.logical_not(has_later))
    def _():
        relay_in[...] = jnp.zeros_like(relay_in)

    pl.semaphore_wait(barrier, len(partners) + has_old.astype(jnp.int32) + has_later.astype(jnp.int32))

    started = []

    def remote(src, dst, send_sem, recv_sem, device):
        return pltpu.make_async_remote_copy(
            src_ref=src, dst_ref=dst, send_sem=send_sem, recv_sem=recv_sem, device_id=device, device_id_type=MESH
        )

    def push(src, dst, recv_sem, device):
        copy = remote(src, dst, send.at[len(started)], recv_sem, device)
        copy.start()
        started.append(copy)

    for part, ref in enumerate((k_ref, v_ref)):
        for d in range(HEADS):
            h = row_at(d)
            src = ref.at[:, pl.ds(pl.multiple_of(h * WIDTH, WIDTH), WIDTH)]
            slot = pl.ds(pl.multiple_of(y * BLOCK, BLOCK), BLOCK)
            push(src, far_in.at[part, slot], far_sem, place(1, h))
            if d == 0:
                pltpu.make_async_copy(src, own_in.at[part, slot], own_sem).start()
            else:
                push(src, own_in.at[part, slot], own_sem, place(0, h))
    for pair in range(2):
        for part, ref in enumerate((q_ref, g_ref)):
            for d in range(HEADS):
                h = row_at(d)
                cols = pl.ds(pl.multiple_of(h * SHARE * WIDTH + pair * PAIR, PAIR), PAIR)
                dst = qg[pair].at[y, part]
                if d == 0:
                    pltpu.make_async_copy(ref.at[:, cols], dst, q_sem.at[pair]).start()
                else:
                    push(ref.at[:, cols], dst, q_sem.at[pair], place(0, h))

    wait(own_in, own_sem)
    forward = remote(own_in, old_in, send.at[46], old_sem, place(2, y))

    @pl.when(has_later)
    def _():
        forward.start()

    kv[:, HALF : 2 * HALF] = own_in[...]
    kt[:, HALF : 2 * HALF] = own_in[0].T

    @pl.when(has_old)
    def _():
        wait(old_in, old_sem)

    kv[:, 0:HALF] = old_in[...]
    kt[:, 0:HALF] = old_in[0].T

    row = lax.broadcasted_iota(jnp.int32, (CHUNK, PAIR), 0)
    token = lax.rem(lax.broadcasted_iota(jnp.int32, (CHUNK, PAIR), 1), WIDTH)

    def unpack(pair):
        for j in range(HEADS):
            for part in range(2):
                x = qg[pair][j, part]
                rows_of[pair, part, j * PAIR : (j + 1) * PAIR] = jnp.concatenate([x[:, :WIDTH], x[:, WIDTH:]], axis=0)

    def unit(pair, i, k):
        j = 2 * i + k
        rows = pl.ds(pl.multiple_of(j * PAIR, PAIR), PAIR)
        return j, 2 * pair + i, rows_of[pair, 0, rows], rows_of[pair, 1, rows]

    def first_of(j):
        line = starts[pl.ds(j, 1)]
        return jnp.concatenate([line, line], axis=1)

    def softmax(first, chunks, base, e, p, diagonal):
        top = jnp.full((8, PAIR), FILL, jnp.float32)
        for c in range(chunks):
            rows = slice(c * CHUNK, (c + 1) * CHUNK)
            keep = row >= first - base(c)
            if diagonal and c >= chunks - BLOCK // CHUNK:
                keep = keep & (row + (c * CHUNK) % BLOCK <= token)
            s = jnp.where(keep, e[rows], FILL)
            e[rows] = s
            top = jnp.maximum(top, fold(s, jnp.max))
        top = jnp.max(top, axis=0, keepdims=True)
        total = jnp.zeros((8, PAIR), jnp.float32)
        delta = jnp.zeros((8, PAIR), jnp.float32)
        for c in range(chunks):
            rows = slice(c * CHUNK, (c + 1) * CHUNK)
            x = jnp.exp((e[rows] - top) * SCALE)
            e[rows] = x
            total = total + fold(x, jnp.sum)
            delta = delta + fold(x * p[rows], jnp.sum)
        return top, jnp.sum(total, axis=0, keepdims=True), jnp.sum(delta, axis=0, keepdims=True)

    def near_scores(pair, i, _):
        units = [unit(pair, i, k) for k in range(2)]
        for k, (j, u, q, g) in enumerate(units):
            keys = pl.ds(pl.multiple_of(j * BLOCK, BLOCK), NEAR)
            e1[k][u] = contract_last(kv[0, keys], q)
            p1[k][u] = contract_last(kv[1, keys], g)
        for k, (j, u, q, g) in enumerate(units):

            def base(c):
                block = j + c * CHUNK // BLOCK
                start = jnp.where(block < HEADS, block * BLOCK - 2 * HALF, (block - HEADS) * BLOCK)
                return start + (c * CHUNK) % BLOCK

            top, total, delta = softmax(first_of(j), NEAR // CHUNK, base, e1[k].at[u], p1[k].at[u], True)
            stat[k][u, 0:1] = top
            stat[k][u, 1:2] = total
            stat[k][u, 2:3] = delta
        return 0

    def far_work(pair, i, _):
        units = [unit(pair, i, k) for k in range(2)]
        for k, (j, u, q, g) in enumerate(units):
            e2[k][...] = contract_last(far_in[0], q)
            p2[k][...] = contract_last(far_in[1], g)
        for k, (j, u, q, g) in enumerate(units):
            top2, total2, delta2 = softmax(first_of(j), HALF // CHUNK, lambda c: c * CHUNK - HALF, e2[k], p2[k], False)
            top1, total1, delta1 = stat[k][u, 0:1], stat[k][u, 1:2], stat[k][u, 2:3]
            top = jnp.maximum(top1, top2)
            a1 = jnp.exp((top1 - top) * SCALE)
            a2 = jnp.exp((top2 - top) * SCALE)
            inverse = 1.0 / (a1 * total1 + a2 * total2)
            delta = (a1 * delta1 + a2 * delta2) * inverse
            a2 = a2 * inverse
            stat[k][u, 0:1] = a1 * inverse
            stat[k][u, 1:2] = delta
            cols = pl.ds(pl.multiple_of(j * PAIR, PAIR), PAIR)
            for c in range(HALF // CHUNK):
                rows = slice(c * CHUNK, (c + 1) * CHUNK)
                p = e2[k][rows] * a2
                ds_far[rows, cols] = (p * (p2[k][rows] - delta)).astype(jnp.bfloat16)
                pr_far[rows, cols] = p.astype(jnp.bfloat16)
        for k, (j, u, q, g) in enumerate(units):
            cols = pl.ds(pl.multiple_of(j * PAIR, PAIR), PAIR)
            dqt[k][u] = matmul(kt_far[...], ds_far[:, cols])
        return 0

    def near_work(pair, i, _):
        units = [unit(pair, i, k) for k in range(2)]
        for k, (j, u, q, g) in enumerate(units):
            a1, delta = stat[k][u, 0:1], stat[k][u, 1:2]
            for c in range(NEAR // CHUNK):
                rows = slice(c * CHUNK, (c + 1) * CHUNK)
                p = e1[k][u, rows] * a1
                ds1[k][rows] = (p * (p1[k][u, rows] - delta)).astype(jnp.bfloat16)
                pr1[k][rows] = p.astype(jnp.bfloat16)
        for k, (j, u, q, g) in enumerate(units):
            keys = pl.ds(pl.multiple_of(j * BLOCK, BLOCK), NEAR)
            acc1[0, keys] += matmul(ds1[k][...], q)
            acc1[1, keys] += matmul(pr1[k][...], g)
            total = dqt[k][u] + matmul(kt[:, keys], ds1[k][...])
            total = (total * SCALE).T.astype(jnp.bfloat16)
            dqs[pair][j] = jnp.concatenate([total[:BLOCK], total[BLOCK:]], axis=1)
        return 0

    def loop(body, pair):
        lax.fori_loop(0, 2, functools.partial(body, pair), 0)

    for pair in range(2):
        wait(qg[pair], q_sem.at[pair])
        unpack(pair)
        loop(near_scores, pair)
        if pair == 0:
            wait(far_in, far_sem)
            kt_far[...] = far_in[0].T
        loop(far_work, pair)
        dk_far = matmul(ds_far[...], rows_of[pair, 0])
        dv_far = matmul(pr_far[...], rows_of[pair, 1])
        if pair == 0:
            acc2[0] = dk_far
            acc2[1] = dv_far
        else:
            far_out[0] = (acc2[0] + dk_far).astype(jnp.bfloat16)
            far_out[1] = (acc2[1] + dv_far).astype(jnp.bfloat16)

    mine = pl.ds(pl.multiple_of(y * WIDTH, WIDTH), WIDTH)
    for d in range(HEADS):
        j = row_at(d)
        rows = pl.ds(pl.multiple_of(j * BLOCK, BLOCK), BLOCK)
        push(far_out.at[:, rows], back.at[1, :, :, mine], back_sem.at[1], place(-1, j))

    for pair in range(2):
        loop(near_work, pair)
        dst = dq_ref.at[:, pl.ds(pl.multiple_of(y * SHARE * WIDTH + pair * PAIR, PAIR), PAIR)]
        for d in range(HEADS):
            j = row_at(d)
            if d == 0:
                pltpu.make_async_copy(dqs[pair].at[j], dst, dq_sem).start()
            else:
                push(dqs[pair].at[j], dst, dq_sem, place(0, j))

    relay_out[...] = acc1[:, 0:HALF].astype(jnp.bfloat16)
    backward = remote(relay_out, relay_in, send.at[47], relay_sem, place(-2, y))

    @pl.when(has_old)
    def _():
        backward.start()

    @pl.when(has_later)
    def _():
        wait(relay_in, relay_sem)

    own_out[...] = (acc1[:, HALF : 2 * HALF] + relay_in[...].astype(jnp.float32)).astype(jnp.bfloat16)
    for d in range(HEADS):
        j = row_at(d)
        rows = pl.ds(pl.multiple_of(j * BLOCK, BLOCK), BLOCK)
        if d == 0:
            pltpu.make_async_copy(own_out.at[:, rows], back.at[0, :, :, mine], back_sem.at[0]).start()
        else:
            push(own_out.at[:, rows], back.at[0, :, :, mine], back_sem.at[0], place(0, j))
    wait(back.at[0], back_sem.at[0])
    wait(back.at[1], back_sem.at[1])
    dk_ref[...] = ((back[0, 0].astype(jnp.float32) + back[1, 0].astype(jnp.float32)) * SCALE).astype(jnp.bfloat16)
    dv_ref[...] = (back[0, 1].astype(jnp.float32) + back[1, 1].astype(jnp.float32)).astype(jnp.bfloat16)
    wait(dq_ref, dq_sem)
    for copy in started:
        copy.wait_send()

    @pl.when(has_later)
    def _():
        forward.wait_send()

    @pl.when(has_old)
    def _():
        backward.wait_send()


def local(queries, key_vectors, value_vectors, output_gradient, doc_lengths):
    low, full = jnp.bfloat16, jnp.float32
    wide = jax.ShapeDtypeStruct((BLOCK, HEADS * SHARE * WIDTH), low)
    narrow = jax.ShapeDtypeStruct((BLOCK, HEADS * WIDTH), low)
    anywhere = pl.BlockSpec(memory_space=pl.ANY)
    near = pl.BlockSpec(memory_space=pltpu.VMEM)
    return pl.pallas_call(
        kernel,
        out_shape=(wide, narrow, narrow),
        in_specs=[anywhere] * 4 + [pl.BlockSpec(memory_space=pltpu.SMEM)],
        out_specs=(anywhere, near, near),
        scratch_shapes=[
            pltpu.VMEM((2, 2 * HALF, WIDTH), low),
            pltpu.VMEM((2, HALF, WIDTH), low),
            pltpu.VMEM((2, HALF, WIDTH), low),
            pltpu.VMEM((2, HALF, WIDTH), low),
            pltpu.VMEM((WIDTH, 2 * HALF), low),
            pltpu.VMEM((WIDTH, HALF), low),
            pltpu.VMEM((HEADS, 2, BLOCK, PAIR), low),
            pltpu.VMEM((HEADS, 2, BLOCK, PAIR), low),
            pltpu.VMEM((2, 2, HEADS * PAIR, WIDTH), low),
            pltpu.VMEM((8, WIDTH), jnp.int32),
            pltpu.VMEM((4, NEAR, PAIR), full),
            pltpu.VMEM((4, NEAR, PAIR), full),
            pltpu.VMEM((4, NEAR, PAIR), full),
            pltpu.VMEM((4, NEAR, PAIR), full),
            pltpu.VMEM((HALF, PAIR), full),
            pltpu.VMEM((HALF, PAIR), full),
            pltpu.VMEM((HALF, PAIR), full),
            pltpu.VMEM((HALF, PAIR), full),
            pltpu.VMEM((HALF, HEADS * PAIR), low),
            pltpu.VMEM((HALF, HEADS * PAIR), low),
            pltpu.VMEM((NEAR, PAIR), low),
            pltpu.VMEM((NEAR, PAIR), low),
            pltpu.VMEM((NEAR, PAIR), low),
            pltpu.VMEM((NEAR, PAIR), low),
            pltpu.VMEM((4, 8, PAIR), full),
            pltpu.VMEM((4, 8, PAIR), full),
            pltpu.VMEM((4, WIDTH, PAIR), full),
            pltpu.VMEM((4, WIDTH, PAIR), full),
            pltpu.VMEM((2, 2 * HALF, WIDTH), full),
            pltpu.VMEM((2, HALF, WIDTH), full),
            pltpu.VMEM((HEADS, BLOCK, PAIR), low),
            pltpu.VMEM((HEADS, BLOCK, PAIR), low),
            pltpu.VMEM((2, HALF, WIDTH), low),
            pltpu.VMEM((2, HALF, WIDTH), low),
            pltpu.VMEM((2, HALF, WIDTH), low),
            pltpu.VMEM((2, HALF, WIDTH), low),
            pltpu.VMEM((2, 2, BLOCK, HEADS * WIDTH), low),
            pltpu.SemaphoreType.DMA((48,)),
            pltpu.SemaphoreType.DMA,
            pltpu.SemaphoreType.DMA,
            pltpu.SemaphoreType.DMA,
            pltpu.SemaphoreType.DMA((2,)),
            pltpu.SemaphoreType.DMA,
            pltpu.SemaphoreType.DMA((2,)),
            pltpu.SemaphoreType.DMA,
        ],
        compiler_params=pltpu.CompilerParams(
            collective_id=0, has_side_effects=True, vmem_limit_bytes=60 << 20
        ),
        cost_estimate=pl.CostEstimate(flops=3 << 30, bytes_accessed=3 << 20, transcendentals=3 << 20),
    )(queries, key_vectors, value_vectors, output_gradient, doc_lengths)


def solution(mesh):
    rows = P(("pb", "kv"), None)
    return jax.shard_map(
        local, mesh=mesh, in_specs=(rows, rows, rows, rows, P()), out_specs=(rows, rows, rows), check_vma=False
    )
```

time: 63.6 us -> 57.1 us (0.90)
  the two profiles are of different devices: /device:TPU:103 before, /device:TPU:7 now
where the time goes in v2:
time: 57.1 us; the launch traced here: 57 us
  Pallas kernels  52.8 us (92%)
  local copies, waits for them, and re-layouts  3.53 us (6%)
  between operations  0.65 us (1%)
    pallas_call x1, Pallas kernels, local(): pl.pallas_call(kernel, out_shape=(wide, narrow, narrow), in_specs=[anywhe...  52.8 us
    unnamed x7, local copies, waits for them, and re-layouts  3.53 us

profile of v2, /device:TPU:7, one launch (start us, length us, event | category | flops | bytes accessed | tf_op | source)
XLA Modules:
  0.0 57.0 jit_solution(1038386029490528247)
XLA Ops:
  0.6 52.8 %shard_map.76 = (bf16[128,2048]{1,0:T(8,128)(2,1)}, bf16[128,512]{1,0:T(8,128)(2,1)}, bf16[128,512]{1,0:T(8,128)(2,1)}) custom-call(bf16[128,2048]{1,0:T(8,128)(2,1)} %q_ref.1, bf16[128,512]{1,0:T(8,128)(2,1)} %k_ref.1, bf16[128,512]{1,0:T(8,128)(2,1)} %v_ref.1, bf16[128,2048]{1,0:T(8,128)(2,1)} %g_ref.1, s32[48]{0:T(128)} %len_ref.1), custom_call_target="tpu_custom_call" | custom-call | flops 3221225472 | bytes 3145728 | tf_op jit(solution)/shard_map/pallas_call | solution.py:335
  53.4 0.0 copy-start.1
  53.4 1.9 %copy.11 = bf16[128,2048]{1,0:T(8,128)(2,1)} copy(bf16[128,2048]{1,0:T(8,128)(2,1)} %get-tuple-element.6) | data formatting | bytes 1048576
  55.4 0.0 copy-done.1
  55.4 0.0 copy-start
  55.4 0.7 %copy.12 = bf16[128,512]{1,0:T(8,128)(2,1)} copy(bf16[128,512]{1,0:T(8,128)(2,1)S(1)} %copy-done.1) | data formatting | bytes 262144
  56.0 0.3 copy-done
  56.3 0.7 %copy.13 = bf16[128,512]{1,0:T(8,128)(2,1)} copy(bf16[128,512]{1,0:T(8,128)(2,1)S(1)} %copy-done) | data formatting | bytes 262144
Async XLA Ops:
  53.4 1.9 %copy-start.1 = (bf16[128,512]{1,0:T(8,128)(2,1)S(1)}, bf16[128,512]{1,0:T(8,128)(2,1)}, u32[]{:S(2)}) copy-start(bf16[128,512]{1,0:T(8,128)(2,1)} %get-tuple-element.7) | copy-start | bytes 393220
  55.4 1.0 %copy-start = (bf16[128,512]{1,0:T(8,128)(2,1)S(1)}, bf16[128,512]{1,0:T(8,128)(2,1)}, u32[]{:S(2)}) copy-start(bf16[128,512]{1,0:T(8,128)(2,1)} %get-tuple-element.8) | copy-start | bytes 393220

commit v3 on v2

--- a/solution.py
+++ b/solution.py
@@ -39,14 +39,15 @@
 
 def kernel(
     q_ref, k_ref, v_ref, g_ref, len_ref,
-    dq_ref, dk_ref, dv_ref,
-    kv, own_in, far_in, old_in, kt, kt_far, qg0, qg1, rows_of, starts,
-    e1a, e1b, p1a, p1b, e2a, e2b, p2a, p2b, ds_far, pr_far, ds1a, ds1b, pr1a, pr1b,
-    stat_a, stat_b, dqt_a, dqt_b, acc1, acc2, dqs0, dqs1, far_out, relay_out, relay_in, own_out, back,
+    dq_ref, back,
+    kv, own_in, far_k, far_v, old_in, kt, kt_far, q0, g0, q1, g1, rows_of, starts,
+    e1a, e1b, p1a, p1b, e2a, e2b, p2a, p2b, ds_fa, ds_fb, pr_fa, pr_fb, ds1a, ds1b, pr1a, pr1b,
+    stat_a, stat_b, dqt_a, dqt_b, acc1, acc2, dqs0, dqs1, far_out, relay_out, relay_in, own_out,
     send, own_sem, far_sem, old_sem, q_sem, relay_sem, back_sem, dq_sem,
 ):
-    qg, dqs, e1, p1, e2, p2 = (qg0, qg1), (dqs0, dqs1), (e1a, e1b), (p1a, p1b), (e2a, e2b), (p2a, p2b)
+    qg, dqs, e1, p1, e2, p2 = ((q0, g0), (q1, g1)), (dqs0, dqs1), (e1a, e1b), (p1a, p1b), (e2a, e2b), (p2a, p2b)
     ds1, pr1, stat, dqt = (ds1a, ds1b), (pr1a, pr1b), (stat_a, stat_b), (dqt_a, dqt_b)
+    ds_far, pr_far = (ds_fa, ds_fb), (pr_fa, pr_fb)
     pb, column = lax.axis_index("pb"), lax.axis_index("kv")
     half = 2 * pb + column // HEADS
     y = lax.rem(column, HEADS)
@@ -118,7 +119,8 @@
             h = row_at(d)
             src = ref.at[:, pl.ds(pl.multiple_of(h * WIDTH, WIDTH), WIDTH)]
             slot = pl.ds(pl.multiple_of(y * BLOCK, BLOCK), BLOCK)
-            push(src, far_in.at[part, slot], far_sem, place(1, h))
+            if part == 0:
+                push(src, far_k.at[slot], far_sem.at[0], place(1, h))
             if d == 0:
                 pltpu.make_async_copy(src, own_in.at[part, slot], own_sem).start()
             else:
@@ -128,11 +130,11 @@
             for d in range(HEADS):
                 h = row_at(d)
                 cols = pl.ds(pl.multiple_of(h * SHARE * WIDTH + pair * PAIR, PAIR), PAIR)
-                dst = qg[pair].at[y, part]
+                dst, sem = qg[pair][part].at[y], q_sem.at[2 * pair + part]
                 if d == 0:
-                    pltpu.make_async_copy(ref.at[:, cols], dst, q_sem.at[pair]).start()
+                    pltpu.make_async_copy(ref.at[:, cols], dst, sem).start()
                 else:
-                    push(ref.at[:, cols], dst, q_sem.at[pair], place(0, h))
+                    push(ref.at[:, cols], dst, sem, place(0, h))
 
     wait(own_in, own_sem)
     forward = remote(own_in, old_in, send.at[46], old_sem, place(2, y))
@@ -141,6 +143,7 @@
     def _():
         forward.start()
 
+    push(own_in.at[1], far_v, far_sem.at[1], place(1, y))
     kv[:, HALF : 2 * HALF] = own_in[...]
     kt[:, HALF : 2 * HALF] = own_in[0].T
 
@@ -154,22 +157,22 @@
     row = lax.broadcasted_iota(jnp.int32, (CHUNK, PAIR), 0)
     token = lax.rem(lax.broadcasted_iota(jnp.int32, (CHUNK, PAIR), 1), WIDTH)
 
-    def unpack(pair):
+    def unpack(pair, part):
+        wait(qg[pair][part], q_sem.at[2 * pair + part])
         for j in range(HEADS):
-            for part in range(2):
-                x = qg[pair][j, part]
-                rows_of[pair, part, j * PAIR : (j + 1) * PAIR] = jnp.concatenate([x[:, :WIDTH], x[:, WIDTH:]], axis=0)
-
-    def unit(pair, i, k):
-        j = 2 * i + k
-        rows = pl.ds(pl.multiple_of(j * PAIR, PAIR), PAIR)
-        return j, 2 * pair + i, rows_of[pair, 0, rows], rows_of[pair, 1, rows]
+            x = qg[pair][part][j]
+            rows = slice(j // 2 * PAIR, (j // 2 + 1) * PAIR)
+            rows_of[pair, part, j % 2, rows] = jnp.concatenate([x[:, :WIDTH], x[:, WIDTH:]], axis=0)
+
+    def units(pair, i):
+        rows = pl.ds(pl.multiple_of(i * PAIR, PAIR), PAIR)
+        return [(k, 2 * i + k, 2 * pair + i, rows_of.at[pair, 0, k, rows], rows_of.at[pair, 1, k, rows]) for k in range(2)]
 
     def first_of(j):
         line = starts[pl.ds(j, 1)]
         return jnp.concatenate([line, line], axis=1)
 
-    def softmax(first, chunks, base, e, p, diagonal):
+    def softmax(first, chunks, base, e, diagonal):
         top = jnp.full((8, PAIR), FILL, jnp.float32)
         for c in range(chunks):
             rows = slice(c * CHUNK, (c + 1) * CHUNK)
@@ -181,74 +184,93 @@
             top = jnp.maximum(top, fold(s, jnp.max))
         top = jnp.max(top, axis=0, keepdims=True)
         total = jnp.zeros((8, PAIR), jnp.float32)
-        delta = jnp.zeros((8, PAIR), jnp.float32)
         for c in range(chunks):
             rows = slice(c * CHUNK, (c + 1) * CHUNK)
             x = jnp.exp((e[rows] - top) * SCALE)
             e[rows] = x
             total = total + fold(x, jnp.sum)
-            delta = delta + fold(x * p[rows], jnp.sum)
-        return top, jnp.sum(total, axis=0, keepdims=True), jnp.sum(delta, axis=0, keepdims=True)
+        return top, jnp.sum(total, axis=0, keepdims=True)
+
+    def weighted(chunks, e, p):
+        delta = jnp.zeros((8, PAIR), jnp.float32)
+        for c in range(chunks):
+            rows = slice(c * CHUNK, (c + 1) * CHUNK)
+            delta = delta + fold(e[rows] * p[rows], jnp.sum)
+        return jnp.sum(delta, axis=0, keepdims=True)
 
     def near_scores(pair, i, _):
-        units = [unit(pair, i, k) for k in range(2)]
-        for k, (j, u, q, g) in enumerate(units):
+        for k, j, u, q, g in units(pair, i):
             keys = pl.ds(pl.multiple_of(j * BLOCK, BLOCK), NEAR)
-            e1[k][u] = contract_last(kv[0, keys], q)
-            p1[k][u] = contract_last(kv[1, keys], g)
-        for k, (j, u, q, g) in enumerate(units):
+            e1[k][u] = contract_last(kv[0, keys], q[...])
+        for k, j, u, q, g in units(pair, i):
 
             def base(c):
                 block = j + c * CHUNK // BLOCK
                 start = jnp.where(block < HEADS, block * BLOCK - 2 * HALF, (block - HEADS) * BLOCK)
                 return start + (c * CHUNK) % BLOCK
 
-            top, total, delta = softmax(first_of(j), NEAR // CHUNK, base, e1[k].at[u], p1[k].at[u], True)
+            top, total = softmax(first_of(j), NEAR // CHUNK, base, e1[k].at[u], True)
             stat[k][u, 0:1] = top
             stat[k][u, 1:2] = total
-            stat[k][u, 2:3] = delta
-        return 0
-
-    def far_work(pair, i, _):
-        units = [unit(pair, i, k) for k in range(2)]
-        for k, (j, u, q, g) in enumerate(units):
-            e2[k][...] = contract_last(far_in[0], q)
-            p2[k][...] = contract_last(far_in[1], g)
-        for k, (j, u, q, g) in enumerate(units):
-            top2, total2, delta2 = softmax(first_of(j), HALF // CHUNK, lambda c: c * CHUNK - HALF, e2[k], p2[k], False)
-            top1, total1, delta1 = stat[k][u, 0:1], stat[k][u, 1:2], stat[k][u, 2:3]
+        return 0
+
+    def far_scores(pair, i, _):
+        for k, j, u, q, g in units(pair, i):
+            e2[k][i] = contract_last(far_k[...], q[...])
+        for k, j, u, q, g in units(pair, i):
+            top, total = softmax(first_of(j), HALF // CHUNK, lambda c: c * CHUNK - HALF, e2[k].at[i], False)
+            stat[k][u, 2:3] = top
+            stat[k][u, 3:4] = total
+        return 0
+
+    def near_values(pair, i, _):
+        for k, j, u, q, g in units(pair, i):
+            keys = pl.ds(pl.multiple_of(j * BLOCK, BLOCK), NEAR)
+            p1[k][u] = contract_last(kv[1, keys], g[...])
+        for k, j, u, q, g in units(pair, i):
+            stat[k][u, 4:5] = weighted(NEAR // CHUNK, e1[k].at[u], p1[k].at[u])
+        return 0
+
+    def far_values(pair, i, _):
+        cols = pl.ds(pl.multiple_of(i * PAIR, PAIR), PAIR)
+        for k, j, u, q, g in units(pair, i):
+            p2[k][...] = contract_last(far_v[...], g[...])
+        for k, j, u, q, g in units(pair, i):
+            delta2 = weighted(HALF // CHUNK, e2[k].at[i], p2[k])
+            top1, total1, top2, total2, delta1 = [stat[k][u, n : n + 1] for n in range(5)]
             top = jnp.maximum(top1, top2)
             a1 = jnp.exp((top1 - top) * SCALE)
             a2 = jnp.exp((top2 - top) * SCALE)
             inverse = 1.0 / (a1 * total1 + a2 * total2)
             delta = (a1 * delta1 + a2 * delta2) * inverse
             a2 = a2 * inverse
-            stat[k][u, 0:1] = a1 * inverse
-            stat[k][u, 1:2] = delta
-            cols = pl.ds(pl.multiple_of(j * PAIR, PAIR), PAIR)
+            stat[k][u, 5:6] = a1 * inverse
+            stat[k][u, 6:7] = delta
             for c in range(HALF // CHUNK):
                 rows = slice(c * CHUNK, (c + 1) * CHUNK)
-                p = e2[k][rows] * a2
-                ds_far[rows, cols] = (p * (p2[k][rows] - delta)).astype(jnp.bfloat16)
-                pr_far[rows, cols] = p.astype(jnp.bfloat16)
-        for k, (j, u, q, g) in enumerate(units):
-            cols = pl.ds(pl.multiple_of(j * PAIR, PAIR), PAIR)
-            dqt[k][u] = matmul(kt_far[...], ds_far[:, cols])
+                p = e2[k][i, rows] * a2
+                ds_far[k][rows, cols] = (p * (p2[k][rows] - delta)).astype(jnp.bfloat16)
+                pr_far[k][rows, cols] = p.astype(jnp.bfloat16)
+        return 0
+
+    def far_queries(pair, i, _):
+        cols = pl.ds(pl.multiple_of(i * PAIR, PAIR), PAIR)
+        for k, j, u, q, g in units(pair, i):
+            dqt[k][u] = matmul(kt_far[...], ds_far[k][:, cols])
         return 0
 
     def near_work(pair, i, _):
-        units = [unit(pair, i, k) for k in range(2)]
-        for k, (j, u, q, g) in enumerate(units):
-            a1, delta = stat[k][u, 0:1], stat[k][u, 1:2]
+        for k, j, u, q, g in units(pair, i):
+            a1, delta = stat[k][u, 5:6], stat[k][u, 6:7]
             for c in range(NEAR // CHUNK):
                 rows = slice(c * CHUNK, (c + 1) * CHUNK)
                 p = e1[k][u, rows] * a1
                 ds1[k][rows] = (p * (p1[k][u, rows] - delta)).astype(jnp.bfloat16)
                 pr1[k][rows] = p.astype(jnp.bfloat16)
-        for k, (j, u, q, g) in enumerate(units):
+        for k, j, u, q, g in units(pair, i):
             keys = pl.ds(pl.multiple_of(j * BLOCK, BLOCK), NEAR)
-            acc1[0, keys] += matmul(ds1[k][...], q)
-            acc1[1, keys] += matmul(pr1[k][...], g)
+            acc1[0, keys] += matmul(ds1[k][...], q[...])
+            acc1[1, keys] += matmul(pr1[k][...], g[...])
             total = dqt[k][u] + matmul(kt[:, keys], ds1[k][...])
             total = (total * SCALE).T.astype(jnp.bfloat16)
             dqs[pair][j] = jnp.concatenate([total[:BLOCK], total[BLOCK:]], axis=1)
@@ -258,15 +280,24 @@
         lax.fori_loop(0, 2, functools.partial(body, pair), 0)
 
     for pair in range(2):
-        wait(qg[pair], q_sem.at[pair])
-        unpack(pair)
+        unpack(pair, 0)
         loop(near_scores, pair)
         if pair == 0:
-            wait(far_in, far_sem)
-            kt_far[...] = far_in[0].T
-        loop(far_work, pair)
-        dk_far = matmul(ds_far[...], rows_of[pair, 0])
-        dv_far = matmul(pr_far[...], rows_of[pair, 1])
+            unpack(pair, 1)
+            loop(near_values, pair)
+            wait(far_k, far_sem.at[0])
+            kt_far[...] = far_k[...].T
+            loop(far_scores, pair)
+            wait(far_v, far_sem.at[1])
+        else:
+            loop(far_scores, pair)
+            unpack(pair, 1)
+            loop(near_values, pair)
+        loop(far_values, pair)
+        if pair == 0:
+            loop(far_queries, pair)
+        dk_far = matmul(ds_fa[...], rows_of[pair, 0, 0]) + matmul(ds_fb[...], rows_of[pair, 0, 1])
+        dv_far = matmul(pr_fa[...], rows_of[pair, 1, 0]) + matmul(pr_fb[...], rows_of[pair, 1, 1])
         if pair == 0:
             acc2[0] = dk_far
             acc2[1] = dv_far
@@ -280,6 +311,7 @@
         rows = pl.ds(pl.multiple_of(j * BLOCK, BLOCK), BLOCK)
         push(far_out.at[:, rows], back.at[1, :, :, mine], back_sem.at[1], place(-1, j))
 
+    loop(far_queries, 1)
     for pair in range(2):
         loop(near_work, pair)
         dst = dq_ref.at[:, pl.ds(pl.multiple_of(y * SHARE * WIDTH + pair * PAIR, PAIR), PAIR)]
@@ -311,8 +343,6 @@
             push(own_out.at[:, rows], back.at[0, :, :, mine], back_sem.at[0], place(0, j))
     wait(back.at[0], back_sem.at[0])
     wait(back.at[1], back_sem.at[1])
-    dk_ref[...] = ((back[0, 0].astype(jnp.float32) + back[1, 0].astype(jnp.float32)) * SCALE).astype(jnp.bfloat16)
-    dv_ref[...] = (back[0, 1].astype(jnp.float32) + back[1, 1].astype(jnp.float32)).astype(jnp.bfloat16)
     wait(dq_ref, dq_sem)
     for copy in started:
         copy.wait_send()
@@ -324,40 +354,53 @@
     @pl.when(has_old)
     def _():
         backward.wait_send()
+
+
+def finish(dq_in, back, dq_ref, dk_ref, dv_ref):
+    dq_ref[...] = dq_in[...]
+    total = back[0].astype(jnp.float32) + back[1].astype(jnp.float32)
+    dk_ref[...] = (total[0] * SCALE).astype(jnp.bfloat16)
+    dv_ref[...] = total[1].astype(jnp.bfloat16)
 
 
 def local(queries, key_vectors, value_vectors, output_gradient, doc_lengths):
     low, full = jnp.bfloat16, jnp.float32
     wide = jax.ShapeDtypeStruct((BLOCK, HEADS * SHARE * WIDTH), low)
     narrow = jax.ShapeDtypeStruct((BLOCK, HEADS * WIDTH), low)
+    shares = jax.ShapeDtypeStruct((2, 2, BLOCK, HEADS * WIDTH), low)
     anywhere = pl.BlockSpec(memory_space=pl.ANY)
     near = pl.BlockSpec(memory_space=pltpu.VMEM)
-    return pl.pallas_call(
+    query_grad, back = pl.pallas_call(
         kernel,
-        out_shape=(wide, narrow, narrow),
+        out_shape=(wide, shares),
         in_specs=[anywhere] * 4 + [pl.BlockSpec(memory_space=pltpu.SMEM)],
-        out_specs=(anywhere, near, near),
+        out_specs=(anywhere, anywhere),
         scratch_shapes=[
             pltpu.VMEM((2, 2 * HALF, WIDTH), low),
             pltpu.VMEM((2, HALF, WIDTH), low),
-            pltpu.VMEM((2, HALF, WIDTH), low),
+            pltpu.VMEM((HALF, WIDTH), low),
+            pltpu.VMEM((HALF, WIDTH), low),
             pltpu.VMEM((2, HALF, WIDTH), low),
             pltpu.VMEM((WIDTH, 2 * HALF), low),
             pltpu.VMEM((WIDTH, HALF), low),
-            pltpu.VMEM((HEADS, 2, BLOCK, PAIR), low),
-            pltpu.VMEM((HEADS, 2, BLOCK, PAIR), low),
-            pltpu.VMEM((2, 2, HEADS * PAIR, WIDTH), low),
+            pltpu.VMEM((HEADS, BLOCK, PAIR), low),
+            pltpu.VMEM((HEADS, BLOCK, PAIR), low),
+            pltpu.VMEM((HEADS, BLOCK, PAIR), low),
+            pltpu.VMEM((HEADS, BLOCK, PAIR), low),
+            pltpu.VMEM((2, 2, 2, 2 * PAIR, WIDTH), low),
             pltpu.VMEM((8, WIDTH), jnp.int32),
             pltpu.VMEM((4, NEAR, PAIR), full),
             pltpu.VMEM((4, NEAR, PAIR), full),
             pltpu.VMEM((4, NEAR, PAIR), full),
             pltpu.VMEM((4, NEAR, PAIR), full),
+            pltpu.VMEM((2, HALF, PAIR), full),
+            pltpu.VMEM((2, HALF, PAIR), full),
             pltpu.VMEM((HALF, PAIR), full),
             pltpu.VMEM((HALF, PAIR), full),
-            pltpu.VMEM((HALF, PAIR), full),
-            pltpu.VMEM((HALF, PAIR), full),
-            pltpu.VMEM((HALF, HEADS * PAIR), low),
-            pltpu.VMEM((HALF, HEADS * PAIR), low),
+            pltpu.VMEM((HALF, 2 * PAIR), low),
+            pltpu.VMEM((HALF, 2 * PAIR), low),
+            pltpu.VMEM((HALF, 2 * PAIR), low),
+            pltpu.VMEM((HALF, 2 * PAIR), low),
             pltpu.VMEM((NEAR, PAIR), low),
             pltpu.VMEM((NEAR, PAIR), low),
             pltpu.VMEM((NEAR, PAIR), low),
@@ -374,12 +417,11 @@
             pltpu.VMEM((2, HALF, WIDTH), low),
             pltpu.VMEM((2, HALF, WIDTH), low),
             pltpu.VMEM((2, HALF, WIDTH), low),
-            pltpu.VMEM((2, 2, BLOCK, HEADS * WIDTH), low),
             pltpu.SemaphoreType.DMA((48,)),
             pltpu.SemaphoreType.DMA,
+            pltpu.SemaphoreType.DMA((2,)),
             pltpu.SemaphoreType.DMA,
-            pltpu.SemaphoreType.DMA,
-            pltpu.SemaphoreType.DMA((2,)),
+            pltpu.SemaphoreType.DMA((4,)),
             pltpu.SemaphoreType.DMA,
             pltpu.SemaphoreType.DMA((2,)),
             pltpu.SemaphoreType.DMA,
@@ -389,6 +431,13 @@
         ),
         cost_estimate=pl.CostEstimate(flops=3 << 30, bytes_accessed=3 << 20, transcendentals=3 << 20),
     )(queries, key_vectors, value_vectors, output_gradient, doc_lengths)
+    return pl.pallas_call(
+        finish,
+        out_shape=(wide, narrow, narrow),
+        in_specs=[near, near],
+        out_specs=(near, near, near),
+        compiler_params=pltpu.CompilerParams(vmem_limit_bytes=60 << 20),
+    )(query_grad, back)
 
 
 def solution(mesh):

time: 57.1 us -> 54.3 us (0.951)
  local copies, waits for them, and re-layouts: 3.53 us -> 0 us
  Pallas kernels: 52.8 us -> 53.5 us
    unnamed x7 -> x0, local copies, waits for them, and re-layouts: 3.53 us -> none
    pallas_call x1 -> x2, Pallas kernels: 52.8 us -> 53.5 us  [the longest x1 51.4 us: local(): pl.pallas_call(kernel, out_shape=(wide, shares), in_specs=[anywhere] * 4...]
where the time goes in v3:
time: 54.3 us; the launch traced here: 54.1 us
  Pallas kernels  53.5 us (99%)
  between operations  0.64 us (1%)
    pallas_call x1, Pallas kernels, local(): pl.pallas_call(kernel, out_shape=(wide, shares), in_specs=[anywhere] * 4...  51.4 us
    pallas_call x1, Pallas kernels, local(): pl.pallas_call(finish, out_shape=(wide, narrow, narrow), in_specs=[near,...  2.12 us

profile of v3, /device:TPU:7, one launch (start us, length us, event | category | flops | bytes accessed | tf_op | source)
XLA Modules:
  0.0 54.1 jit_solution(14283427385910867918)
XLA Ops:
  0.6 51.4 %shard_map.76 = (bf16[128,2048]{1,0:T(8,128)(2,1)}, bf16[2,2,128,512]{3,2,1,0:T(8,128)(2,1)}) custom-call(bf16[128,2048]{1,0:T(8,128)(2,1)} %q_ref.1, bf16[128,512]{1,0:T(8,128)(2,1)} %k_ref.1, bf16[128,512]{1,0:T(8,128)(2,1)} %v_ref.1, bf16[128,2048]{1,0:T(8,128)(2,1)} %g_ref.1, s32[48]{0:T(128)} %len_ref.1), custom_call_target="tpu_custom_call" | custom-call | flops 3221225472 | bytes 3145728 | tf_op jit(solution)/shard_map/pallas_call | solution.py:373
  52.0 2.1 %shard_map.77 = (bf16[128,2048]{1,0:T(8,128)(2,1)}, bf16[128,512]{1,0:T(8,128)(2,1)}, bf16[128,512]{1,0:T(8,128)(2,1)}) custom-call(bf16[128,2048]{1,0:T(8,128)(2,1)} %get-tuple-element.5.dq_in, bf16[2,2,128,512]{3,2,1,0:T(8,128)(2,1)} %get-tuple-element.6.back), custom_call_target="tpu_custom_call" | custom-call | tf_op jit(solution)/shard_map/pallas_call | solution.py:434

commit v4 on v3

--- a/solution.py
+++ b/solution.py
@@ -1,5 +1,3 @@
-import functools
-
 import jax
 import jax.numpy as jnp
 from jax import lax
@@ -41,13 +39,15 @@
     q_ref, k_ref, v_ref, g_ref, len_ref,
     dq_ref, back,
     kv, own_in, far_k, far_v, old_in, kt, kt_far, q0, g0, q1, g1, rows_of, starts,
-    e1a, e1b, p1a, p1b, e2a, e2b, p2a, p2b, ds_fa, ds_fb, pr_fa, pr_fb, ds1a, ds1b, pr1a, pr1b,
-    stat_a, stat_b, dqt_a, dqt_b, acc1, acc2, dqs0, dqs1, far_out, relay_out, relay_in, own_out,
+    e1a, e1b, p1a, p1b, e2a, e2b, p2a, p2b, ds_fa, ds_fb, pr_fa, pr_fb, ds_0, ds_1, ds_2, ds_3, pr_0, pr_1, pr_2, pr_3,
+    stat_a, stat_b, dqt_a, dqt_b, acc1, acc2, dqs0, dqs1, far_ok, far_ov, relay_out, relay_in, own_out,
     send, own_sem, far_sem, old_sem, q_sem, relay_sem, back_sem, dq_sem,
 ):
-    qg, dqs, e1, p1, e2, p2 = ((q0, g0), (q1, g1)), (dqs0, dqs1), (e1a, e1b), (p1a, p1b), (e2a, e2b), (p2a, p2b)
-    ds1, pr1, stat, dqt = (ds1a, ds1b), (pr1a, pr1b), (stat_a, stat_b), (dqt_a, dqt_b)
-    ds_far, pr_far = (ds_fa, ds_fb), (pr_fa, pr_fb)
+    dqs = (dqs0, dqs1)
+    qg, e1, p1, e2, p2 = ((q0, g0), (q1, g1)), (e1a, e1b), (p1a, p1b), (e2a, e2b), (p2a, p2b)
+    ds1, pr1 = (ds_0, ds_1, ds_2, ds_3), (pr_0, pr_1, pr_2, pr_3)
+    stat, dqt = (stat_a, stat_b), (dqt_a, dqt_b)
+    ds_far, pr_far, far_out = (ds_fa, ds_fb), (pr_fa, pr_fb), (far_ok, far_ov)
     pb, column = lax.axis_index("pb"), lax.axis_index("kv")
     half = 2 * pb + column // HEADS
     y = lax.rem(column, HEADS)
@@ -74,31 +74,6 @@
     @pl.when(has_old)
     def _():
         pl.semaphore_signal(barrier, inc=1, device_id=place(-2, y), device_id_type=MESH)
-
-    positions = (
-        lax.broadcasted_iota(jnp.int32, (8, WIDTH), 0) * BLOCK
-        + lax.broadcasted_iota(jnp.int32, (8, WIDTH), 1)
-        + half * HALF
-    )
-
-    def count(i, carry):
-        end, start = carry
-        end = end + len_ref[i]
-        return end, jnp.where(positions >= end, end, start)
-
-    _, doc_start = lax.fori_loop(
-        0, len_ref.shape[0], count, (jnp.int32(0), jnp.zeros((8, WIDTH), jnp.int32))
-    )
-    starts[...] = doc_start - half * HALF
-    acc1[...] = jnp.zeros_like(acc1)
-
-    @pl.when(jnp.logical_not(has_old))
-    def _():
-        old_in[...] = jnp.zeros_like(old_in)
-
-    @pl.when(jnp.logical_not(has_later))
-    def _():
-        relay_in[...] = jnp.zeros_like(relay_in)
 
     pl.semaphore_wait(barrier, len(partners) + has_old.astype(jnp.int32) + has_later.astype(jnp.int32))
 
@@ -136,6 +111,31 @@
                 else:
                     push(ref.at[:, cols], dst, sem, place(0, h))
 
+    positions = (
+        lax.broadcasted_iota(jnp.int32, (8, WIDTH), 0) * BLOCK
+        + lax.broadcasted_iota(jnp.int32, (8, WIDTH), 1)
+        + half * HALF
+    )
+
+    def count(i, carry):
+        end, start = carry
+        end = end + len_ref[i]
+        return end, jnp.where(positions >= end, end, start)
+
+    _, doc_start = lax.fori_loop(
+        0, len_ref.shape[0], count, (jnp.int32(0), jnp.zeros((8, WIDTH), jnp.int32))
+    )
+    starts[...] = doc_start - half * HALF
+    acc1[...] = jnp.zeros_like(acc1)
+
+    @pl.when(jnp.logical_not(has_old))
+    def _():
+        old_in[...] = jnp.zeros_like(old_in)
+
+    @pl.when(jnp.logical_not(has_later))
+    def _():
+        relay_in[...] = jnp.zeros_like(relay_in)
+
     wait(own_in, own_sem)
     forward = remote(own_in, old_in, send.at[46], old_sem, place(2, y))
 
@@ -164,12 +164,20 @@
             rows = slice(j // 2 * PAIR, (j // 2 + 1) * PAIR)
             rows_of[pair, part, j % 2, rows] = jnp.concatenate([x[:, :WIDTH], x[:, WIDTH:]], axis=0)
 
-    def units(pair, i):
-        rows = pl.ds(pl.multiple_of(i * PAIR, PAIR), PAIR)
-        return [(k, 2 * i + k, 2 * pair + i, rows_of.at[pair, 0, k, rows], rows_of.at[pair, 1, k, rows]) for k in range(2)]
+    def unit(pair, j):
+        k, u = j % 2, 2 * pair + j // 2
+        rows = slice(j // 2 * PAIR, (j // 2 + 1) * PAIR)
+        return k, u, rows_of.at[pair, 0, k, rows], rows_of.at[pair, 1, k, rows]
+
+    def staged(ahead, work):
+        ahead(0)
+        for j in range(HEADS):
+            if j + 1 < HEADS:
+                ahead(j + 1)
+            work(j)
 
     def first_of(j):
-        line = starts[pl.ds(j, 1)]
+        line = starts[j : j + 1]
         return jnp.concatenate([line, line], axis=1)
 
     def softmax(first, chunks, base, e, diagonal):
@@ -198,122 +206,129 @@
             delta = delta + fold(e[rows] * p[rows], jnp.sum)
         return jnp.sum(delta, axis=0, keepdims=True)
 
-    def near_scores(pair, i, _):
-        for k, j, u, q, g in units(pair, i):
-            keys = pl.ds(pl.multiple_of(j * BLOCK, BLOCK), NEAR)
-            e1[k][u] = contract_last(kv[0, keys], q[...])
-        for k, j, u, q, g in units(pair, i):
+    def near_scores(pair):
+        def ahead(j):
+            k, u, q, g = unit(pair, j)
+            e1[k][u] = contract_last(kv[0, j * BLOCK : j * BLOCK + NEAR], q[...])
+
+        def work(j):
+            k, u, q, g = unit(pair, j)
 
             def base(c):
                 block = j + c * CHUNK // BLOCK
-                start = jnp.where(block < HEADS, block * BLOCK - 2 * HALF, (block - HEADS) * BLOCK)
+                start = block * BLOCK - 2 * HALF if block < HEADS else (block - HEADS) * BLOCK
                 return start + (c * CHUNK) % BLOCK
 
             top, total = softmax(first_of(j), NEAR // CHUNK, base, e1[k].at[u], True)
             stat[k][u, 0:1] = top
             stat[k][u, 1:2] = total
-        return 0
-
-    def far_scores(pair, i, _):
-        for k, j, u, q, g in units(pair, i):
-            e2[k][i] = contract_last(far_k[...], q[...])
-        for k, j, u, q, g in units(pair, i):
-            top, total = softmax(first_of(j), HALF // CHUNK, lambda c: c * CHUNK - HALF, e2[k].at[i], False)
-            stat[k][u, 2:3] = top
-            stat[k][u, 3:4] = total
-        return 0
-
-    def near_values(pair, i, _):
-        for k, j, u, q, g in units(pair, i):
-            keys = pl.ds(pl.multiple_of(j * BLOCK, BLOCK), NEAR)
-            p1[k][u] = contract_last(kv[1, keys], g[...])
-        for k, j, u, q, g in units(pair, i):
-            stat[k][u, 4:5] = weighted(NEAR // CHUNK, e1[k].at[u], p1[k].at[u])
-        return 0
-
-    def far_values(pair, i, _):
-        cols = pl.ds(pl.multiple_of(i * PAIR, PAIR), PAIR)
-        for k, j, u, q, g in units(pair, i):
-            p2[k][...] = contract_last(far_v[...], g[...])
-        for k, j, u, q, g in units(pair, i):
-            delta2 = weighted(HALF // CHUNK, e2[k].at[i], p2[k])
-            top1, total1, top2, total2, delta1 = [stat[k][u, n : n + 1] for n in range(5)]
+
+        staged(ahead, work)
+
+    def far_scores(pair):
+        def ahead(j):
+            k, u, q, g = unit(pair, j)
+            e2[k][j // 2] = contract_last(far_k[...], q[...])
+
+        def work(j):
+            k, u, q, g = unit(pair, j)
+            i, cols = j // 2, slice(j // 2 * PAIR, (j // 2 + 1) * PAIR)
+            top2, total2 = softmax(first_of(j), HALF // CHUNK, lambda c: c * CHUNK - HALF, e2[k].at[i], False)
+            top1, total1 = stat[k][u, 0:1], stat[k][u, 1:2]
             top = jnp.maximum(top1, top2)
             a1 = jnp.exp((top1 - top) * SCALE)
             a2 = jnp.exp((top2 - top) * SCALE)
             inverse = 1.0 / (a1 * total1 + a2 * total2)
-            delta = (a1 * delta1 + a2 * delta2) * inverse
+            stat[k][u, 5:6] = a1 * inverse
             a2 = a2 * inverse
-            stat[k][u, 5:6] = a1 * inverse
+            for c in range(HALF // CHUNK):
+                rows = slice(c * CHUNK, (c + 1) * CHUNK)
+                p = e2[k][i, rows] * a2
+                e2[k][i, rows] = p
+                pr_far[k][rows, cols] = p.astype(jnp.bfloat16)
+
+        staged(ahead, work)
+
+    def near_values(pair):
+        def ahead(j):
+            k, u, q, g = unit(pair, j)
+            p1[k][u] = contract_last(kv[1, j * BLOCK : j * BLOCK + NEAR], g[...])
+
+        def work(j):
+            k, u, q, g = unit(pair, j)
+            stat[k][u, 4:5] = weighted(NEAR // CHUNK, e1[k].at[u], p1[k].at[u])
+
+        staged(ahead, work)
+
+    def far_values(pair):
+        def ahead(j):
+            k, u, q, g = unit(pair, j)
+            p2[k][j // 2] = contract_last(far_v[...], g[...])
+
+        def work(j):
+            k, u, q, g = unit(pair, j)
+            i, cols = j // 2, slice(j // 2 * PAIR, (j // 2 + 1) * PAIR)
+            delta = stat[k][u, 5:6] * stat[k][u, 4:5] + weighted(HALF // CHUNK, e2[k].at[i], p2[k].at[i])
             stat[k][u, 6:7] = delta
             for c in range(HALF // CHUNK):
                 rows = slice(c * CHUNK, (c + 1) * CHUNK)
-                p = e2[k][i, rows] * a2
-                ds_far[k][rows, cols] = (p * (p2[k][rows] - delta)).astype(jnp.bfloat16)
-                pr_far[k][rows, cols] = p.astype(jnp.bfloat16)
-        return 0
-
-    def far_queries(pair, i, _):
-        cols = pl.ds(pl.multiple_of(i * PAIR, PAIR), PAIR)
-        for k, j, u, q, g in units(pair, i):
-            dqt[k][u] = matmul(kt_far[...], ds_far[k][:, cols])
-        return 0
-
-    def near_work(pair, i, _):
-        for k, j, u, q, g in units(pair, i):
-            a1, delta = stat[k][u, 5:6], stat[k][u, 6:7]
-            for c in range(NEAR // CHUNK):
-                rows = slice(c * CHUNK, (c + 1) * CHUNK)
-                p = e1[k][u, rows] * a1
-                ds1[k][rows] = (p * (p1[k][u, rows] - delta)).astype(jnp.bfloat16)
-                pr1[k][rows] = p.astype(jnp.bfloat16)
-        for k, j, u, q, g in units(pair, i):
-            keys = pl.ds(pl.multiple_of(j * BLOCK, BLOCK), NEAR)
-            acc1[0, keys] += matmul(ds1[k][...], q[...])
-            acc1[1, keys] += matmul(pr1[k][...], g[...])
-            total = dqt[k][u] + matmul(kt[:, keys], ds1[k][...])
+                ds_far[k][rows, cols] = (e2[k][i, rows] * (p2[k][i, rows] - delta)).astype(jnp.bfloat16)
+
+        staged(ahead, work)
+
+    def far_queries(pair):
+        for j in range(HEADS):
+            k, u, q, g = unit(pair, j)
+            dqt[k][u] = matmul(kt_far[...], ds_far[k][:, j // 2 * PAIR : (j // 2 + 1) * PAIR])
+
+    def near_rows(pair, j, low, high):
+        k, u = j % 2, 2 * pair + j // 2
+        a1, delta = stat[k][u, 5:6], stat[k][u, 6:7]
+        for c in range(low // CHUNK, high // CHUNK):
+            rows = slice(c * CHUNK, (c + 1) * CHUNK)
+            p = e1[k][u, rows] * a1
+            ds1[j][pair, rows] = (p * (p1[k][u, rows] - delta)).astype(jnp.bfloat16)
+            pr1[j][rows] = p.astype(jnp.bfloat16)
+
+    def near_keys(pair, j, low, high):
+        keys = slice(j * BLOCK + low, j * BLOCK + high)
+        mine = slice(j // 2 * PAIR, (j // 2 + 1) * PAIR)
+        acc1[0, keys] += matmul(ds1[j][pair, low:high], rows_of[pair, 0, j % 2, mine])
+        acc1[1, keys] += matmul(pr1[j][low:high], rows_of[pair, 1, j % 2, mine])
+
+    def old_work(pair):
+        for j in range(HEADS):
+            near_rows(pair, j, 0, HALF - j * BLOCK)
+        for j in range(HEADS):
+            near_keys(pair, j, 0, HALF - j * BLOCK)
+
+    def own_work(pair):
+        for j in range(HEADS):
+            near_rows(pair, j, HALF - j * BLOCK, NEAR)
+        for j in range(HEADS):
+            near_keys(pair, j, HALF - j * BLOCK, NEAR)
+            k, u = j % 2, 2 * pair + j // 2
+            total = dqt[k][u] + matmul(kt[:, j * BLOCK : j * BLOCK + NEAR], ds1[j][pair])
             total = (total * SCALE).T.astype(jnp.bfloat16)
             dqs[pair][j] = jnp.concatenate([total[:BLOCK], total[BLOCK:]], axis=1)
-        return 0
-
-    def loop(body, pair):
-        lax.fori_loop(0, 2, functools.partial(body, pair), 0)
-
-    for pair in range(2):
-        unpack(pair, 0)
-        loop(near_scores, pair)
+
+    mine = pl.ds(pl.multiple_of(y * WIDTH, WIDTH), WIDTH)
+
+    def send_far(part):
+        for d in range(HEADS):
+            j = row_at(d)
+            rows = pl.ds(pl.multiple_of(j * BLOCK, BLOCK), BLOCK)
+            push(far_out[part].at[rows], back.at[1, part, :, mine], back_sem.at[1], place(-1, j))
+
+    def far_sum(pair, part, left):
+        total = matmul(left[0][...], rows_of[pair, part, 0]) + matmul(left[1][...], rows_of[pair, part, 1])
         if pair == 0:
-            unpack(pair, 1)
-            loop(near_values, pair)
-            wait(far_k, far_sem.at[0])
-            kt_far[...] = far_k[...].T
-            loop(far_scores, pair)
-            wait(far_v, far_sem.at[1])
+            acc2[part] = total
         else:
-            loop(far_scores, pair)
-            unpack(pair, 1)
-            loop(near_values, pair)
-        loop(far_values, pair)
-        if pair == 0:
-            loop(far_queries, pair)
-        dk_far = matmul(ds_fa[...], rows_of[pair, 0, 0]) + matmul(ds_fb[...], rows_of[pair, 0, 1])
-        dv_far = matmul(pr_fa[...], rows_of[pair, 1, 0]) + matmul(pr_fb[...], rows_of[pair, 1, 1])
-        if pair == 0:
-            acc2[0] = dk_far
-            acc2[1] = dv_far
-        else:
-            far_out[0] = (acc2[0] + dk_far).astype(jnp.bfloat16)
-            far_out[1] = (acc2[1] + dv_far).astype(jnp.bfloat16)
-
-    mine = pl.ds(pl.multiple_of(y * WIDTH, WIDTH), WIDTH)
-    for d in range(HEADS):
-        j = row_at(d)
-        rows = pl.ds(pl.multiple_of(j * BLOCK, BLOCK), BLOCK)
-        push(far_out.at[:, rows], back.at[1, :, :, mine], back_sem.at[1], place(-1, j))
-
-    loop(far_queries, 1)
-    for pair in range(2):
-        loop(near_work, pair)
+            far_out[part][...] = (acc2[part] + total).astype(jnp.bfloat16)
+            send_far(part)
+
+    def send_queries(pair):
         dst = dq_ref.at[:, pl.ds(pl.multiple_of(y * SHARE * WIDTH + pair * PAIR, PAIR), PAIR)]
         for d in range(HEADS):
             j = row_at(d)
@@ -322,6 +337,29 @@
             else:
                 push(dqs[pair].at[j], dst, dq_sem, place(0, j))
 
+    for pair in range(2):
+        unpack(pair, 0)
+        near_scores(pair)
+        if pair == 0:
+            unpack(pair, 1)
+            near_values(pair)
+            wait(far_k, far_sem.at[0])
+            kt_far[...] = far_k[...].T
+            far_scores(pair)
+            far_sum(pair, 1, pr_far)
+            wait(far_v, far_sem.at[1])
+        else:
+            far_scores(pair)
+            unpack(pair, 1)
+            far_sum(pair, 1, pr_far)
+            near_values(pair)
+        far_values(pair)
+        if pair == 0:
+            far_queries(pair)
+        far_sum(pair, 0, ds_far)
+
+    old_work(0)
+    old_work(1)
     relay_out[...] = acc1[:, 0:HALF].astype(jnp.bfloat16)
     backward = remote(relay_out, relay_in, send.at[47], relay_sem, place(-2, y))
 
@@ -329,6 +367,11 @@
     def _():
         backward.start()
 
+    own_work(0)
+    send_queries(0)
+    far_queries(1)
+    own_work(1)
+    send_queries(1)
     @pl.when(has_later)
     def _():
         wait(relay_in, relay_sem)
@@ -395,12 +438,16 @@
             pltpu.VMEM((4, NEAR, PAIR), full),
             pltpu.VMEM((2, HALF, PAIR), full),
             pltpu.VMEM((2, HALF, PAIR), full),
-            pltpu.VMEM((HALF, PAIR), full),
-            pltpu.VMEM((HALF, PAIR), full),
+            pltpu.VMEM((2, HALF, PAIR), full),
+            pltpu.VMEM((2, HALF, PAIR), full),
             pltpu.VMEM((HALF, 2 * PAIR), low),
             pltpu.VMEM((HALF, 2 * PAIR), low),
             pltpu.VMEM((HALF, 2 * PAIR), low),
             pltpu.VMEM((HALF, 2 * PAIR), low),
+            pltpu.VMEM((2, NEAR, PAIR), low),
+            pltpu.VMEM((2, NEAR, PAIR), low),
+            pltpu.VMEM((2, NEAR, PAIR), low),
+            pltpu.VMEM((2, NEAR, PAIR), low),
             pltpu.VMEM((NEAR, PAIR), low),
             pltpu.VMEM((NEAR, PAIR), low),
             pltpu.VMEM((NEAR, PAIR), low),
@@ -413,7 +460,8 @@
             pltpu.VMEM((2, HALF, WIDTH), full),
             pltpu.VMEM((HEADS, BLOCK, PAIR), low),
             pltpu.VMEM((HEADS, BLOCK, PAIR), low),
-            pltpu.VMEM((2, HALF, WIDTH), low),
+            pltpu.VMEM((HALF, WIDTH), low),
+            pltpu.VMEM((HALF, WIDTH), low),
             pltpu.VMEM((2, HALF, WIDTH), low),
             pltpu.VMEM((2, HALF, WIDTH), low),
             pltpu.VMEM((2, HALF, WIDTH), low),

time: 54.3 us -> 51.6 us (0.950)
  Pallas kernels: 53.5 us -> 50.9 us
    pallas_call x1, Pallas kernels: 51.4 us -> 48.8 us  [local(): pl.pallas_call(kernel, out_shape=(wide, shares), in_specs=[anywhere] * 4...]
where the time goes in v4:
time: 51.6 us; the launch traced here: 51.5 us
  Pallas kernels  50.9 us (99%)
  between operations  0.64 us (1%)
    pallas_call x1, Pallas kernels, local(): pl.pallas_call(kernel, out_shape=(wide, shares), in_specs=[anywhere] * 4...  48.8 us
    pallas_call x1, Pallas kernels, local(): pl.pallas_call(finish, out_shape=(wide, narrow, narrow), in_specs=[near,...  2.12 us

profile of v4, /device:TPU:7, one launch (start us, length us, event | category | flops | bytes accessed | tf_op | source)
XLA Modules:
  0.0 51.5 jit_solution(10439659858501888310)
XLA Ops:
  0.6 48.8 %shard_map.76 = (bf16[128,2048]{1,0:T(8,128)(2,1)}, bf16[2,2,128,512]{3,2,1,0:T(8,128)(2,1)}) custom-call(bf16[128,2048]{1,0:T(8,128)(2,1)} %q_ref.1, bf16[128,512]{1,0:T(8,128)(2,1)} %k_ref.1, bf16[128,512]{1,0:T(8,128)(2,1)} %v_ref.1, bf16[128,2048]{1,0:T(8,128)(2,1)} %g_ref.1, s32[48]{0:T(128)} %len_ref.1), custom_call_target="tpu_custom_call" | custom-call | flops 3221225472 | bytes 3145728 | tf_op jit(solution)/shard_map/pallas_call | solution.py:416
  49.4 2.1 %shard_map.77 = (bf16[128,2048]{1,0:T(8,128)(2,1)}, bf16[128,512]{1,0:T(8,128)(2,1)}, bf16[128,512]{1,0:T(8,128)(2,1)}) custom-call(bf16[128,2048]{1,0:T(8,128)(2,1)} %get-tuple-element.5.dq_in, bf16[2,2,128,512]{3,2,1,0:T(8,128)(2,1)} %get-tuple-element.6.back), custom_call_target="tpu_custom_call" | custom-call | tf_op jit(solution)/shard_map/pallas_call | solution.py:482

commit v5 on v4

--- a/solution.py
+++ b/solution.py
@@ -89,17 +89,22 @@
         copy.start()
         started.append(copy)
 
+    def share(ref, part, d):
+        h = row_at(d)
+        return h, ref.at[:, pl.ds(pl.multiple_of(h * WIDTH, WIDTH), WIDTH)]
+
+    slot = pl.ds(pl.multiple_of(y * BLOCK, BLOCK), BLOCK)
     for part, ref in enumerate((k_ref, v_ref)):
         for d in range(HEADS):
-            h = row_at(d)
-            src = ref.at[:, pl.ds(pl.multiple_of(h * WIDTH, WIDTH), WIDTH)]
-            slot = pl.ds(pl.multiple_of(y * BLOCK, BLOCK), BLOCK)
-            if part == 0:
-                push(src, far_k.at[slot], far_sem.at[0], place(1, h))
+            h, src = share(ref, part, d)
             if d == 0:
                 pltpu.make_async_copy(src, own_in.at[part, slot], own_sem).start()
             else:
                 push(src, own_in.at[part, slot], own_sem, place(0, h))
+    for ref, far, sem in ((k_ref, far_k, far_sem.at[0]), (v_ref, far_v, far_sem.at[1])):
+        for d in range(HEADS):
+            h, src = share(ref, 0, d)
+            push(src, far.at[slot], sem, place(1, h))
     for pair in range(2):
         for part, ref in enumerate((q_ref, g_ref)):
             for d in range(HEADS):
@@ -143,16 +148,8 @@
     def _():
         forward.start()
 
-    push(own_in.at[1], far_v, far_sem.at[1], place(1, y))
     kv[:, HALF : 2 * HALF] = own_in[...]
     kt[:, HALF : 2 * HALF] = own_in[0].T
-
-    @pl.when(has_old)
-    def _():
-        wait(old_in, old_sem)
-
-    kv[:, 0:HALF] = old_in[...]
-    kt[:, 0:HALF] = old_in[0].T
 
     row = lax.broadcasted_iota(jnp.int32, (CHUNK, PAIR), 0)
     token = lax.rem(lax.broadcasted_iota(jnp.int32, (CHUNK, PAIR), 1), WIDTH)
@@ -180,46 +177,48 @@
         line = starts[j : j + 1]
         return jnp.concatenate([line, line], axis=1)
 
-    def softmax(first, chunks, base, e, diagonal):
+    def softmax(first, pieces):
         top = jnp.full((8, PAIR), FILL, jnp.float32)
-        for c in range(chunks):
-            rows = slice(c * CHUNK, (c + 1) * CHUNK)
-            keep = row >= first - base(c)
-            if diagonal and c >= chunks - BLOCK // CHUNK:
-                keep = keep & (row + (c * CHUNK) % BLOCK <= token)
-            s = jnp.where(keep, e[rows], FILL)
-            e[rows] = s
-            top = jnp.maximum(top, fold(s, jnp.max))
+        for e, rows, base, diagonal in pieces:
+            for r in range(rows.start, rows.stop, CHUNK):
+                part = slice(r, r + CHUNK)
+                keep = row >= first - (base + r - rows.start)
+                if diagonal and r >= rows.stop - BLOCK:
+                    keep = keep & (row + (r - rows.stop + BLOCK) <= token)
+                s = jnp.where(keep, e[part], FILL)
+                e[part] = s
+                top = jnp.maximum(top, fold(s, jnp.max))
         top = jnp.max(top, axis=0, keepdims=True)
         total = jnp.zeros((8, PAIR), jnp.float32)
-        for c in range(chunks):
-            rows = slice(c * CHUNK, (c + 1) * CHUNK)
-            x = jnp.exp((e[rows] - top) * SCALE)
-            e[rows] = x
-            total = total + fold(x, jnp.sum)
+        for e, rows, base, diagonal in pieces:
+            for r in range(rows.start, rows.stop, CHUNK):
+                part = slice(r, r + CHUNK)
+                x = jnp.exp((e[part] - top) * SCALE)
+                e[part] = x
+                total = total + fold(x, jnp.sum)
         return top, jnp.sum(total, axis=0, keepdims=True)
 
-    def weighted(chunks, e, p):
+    def weighted(rows, e, p):
         delta = jnp.zeros((8, PAIR), jnp.float32)
-        for c in range(chunks):
-            rows = slice(c * CHUNK, (c + 1) * CHUNK)
-            delta = delta + fold(e[rows] * p[rows], jnp.sum)
+        for r in range(rows.start, rows.stop, CHUNK):
+            part = slice(r, r + CHUNK)
+            delta = delta + fold(e[part] * p[part], jnp.sum)
         return jnp.sum(delta, axis=0, keepdims=True)
 
-    def near_scores(pair):
+    def old_rows(j):
+        return slice(0, HALF - j * BLOCK)
+
+    def own_rows(j):
+        return slice(HALF - j * BLOCK, NEAR)
+
+    def own_scores(pair):
         def ahead(j):
             k, u, q, g = unit(pair, j)
-            e1[k][u] = contract_last(kv[0, j * BLOCK : j * BLOCK + NEAR], q[...])
+            e1[k][u, own_rows(j)] = contract_last(kv[0, HALF : HALF + (j + 1) * BLOCK], q[...])
 
         def work(j):
             k, u, q, g = unit(pair, j)
-
-            def base(c):
-                block = j + c * CHUNK // BLOCK
-                start = block * BLOCK - 2 * HALF if block < HEADS else (block - HEADS) * BLOCK
-                return start + (c * CHUNK) % BLOCK
-
-            top, total = softmax(first_of(j), NEAR // CHUNK, base, e1[k].at[u], True)
+            top, total = softmax(first_of(j), [(e1[k].at[u], own_rows(j), 0, True)])
             stat[k][u, 0:1] = top
             stat[k][u, 1:2] = total
 
@@ -228,19 +227,25 @@
     def far_scores(pair):
         def ahead(j):
             k, u, q, g = unit(pair, j)
+            e1[k][u, old_rows(j)] = contract_last(kv[0, j * BLOCK : HALF], q[...])
             e2[k][j // 2] = contract_last(far_k[...], q[...])
 
         def work(j):
             k, u, q, g = unit(pair, j)
             i, cols = j // 2, slice(j // 2 * PAIR, (j // 2 + 1) * PAIR)
-            top2, total2 = softmax(first_of(j), HALF // CHUNK, lambda c: c * CHUNK - HALF, e2[k].at[i], False)
+            pieces = [
+                (e1[k].at[u], old_rows(j), j * BLOCK - 2 * HALF, False),
+                (e2[k].at[i], slice(0, HALF), -HALF, False),
+            ]
+            top2, total2 = softmax(first_of(j), pieces)
             top1, total1 = stat[k][u, 0:1], stat[k][u, 1:2]
             top = jnp.maximum(top1, top2)
             a1 = jnp.exp((top1 - top) * SCALE)
             a2 = jnp.exp((top2 - top) * SCALE)
             inverse = 1.0 / (a1 * total1 + a2 * total2)
+            a2 = a2 * inverse
+            stat[k][u, 2:3] = a2
             stat[k][u, 5:6] = a1 * inverse
-            a2 = a2 * inverse
             for c in range(HALF // CHUNK):
                 rows = slice(c * CHUNK, (c + 1) * CHUNK)
                 p = e2[k][i, rows] * a2
@@ -249,14 +254,25 @@
 
         staged(ahead, work)
 
-    def near_values(pair):
+    def own_values(pair):
         def ahead(j):
             k, u, q, g = unit(pair, j)
-            p1[k][u] = contract_last(kv[1, j * BLOCK : j * BLOCK + NEAR], g[...])
+            p1[k][u, own_rows(j)] = contract_last(kv[1, HALF : HALF + (j + 1) * BLOCK], g[...])
 
         def work(j):
             k, u, q, g = unit(pair, j)
-            stat[k][u, 4:5] = weighted(NEAR // CHUNK, e1[k].at[u], p1[k].at[u])
+            stat[k][u, 4:5] = weighted(own_rows(j), e1[k].at[u], p1[k].at[u])
+
+        staged(ahead, work)
+
+    def old_values(pair):
+        def ahead(j):
+            k, u, q, g = unit(pair, j)
+            p1[k][u, old_rows(j)] = contract_last(kv[1, j * BLOCK : HALF], g[...])
+
+        def work(j):
+            k, u, q, g = unit(pair, j)
+            stat[k][u, 3:4] = weighted(old_rows(j), e1[k].at[u], p1[k].at[u])
 
         staged(ahead, work)
 
@@ -268,7 +284,8 @@
         def work(j):
             k, u, q, g = unit(pair, j)
             i, cols = j // 2, slice(j // 2 * PAIR, (j // 2 + 1) * PAIR)
-            delta = stat[k][u, 5:6] * stat[k][u, 4:5] + weighted(HALF // CHUNK, e2[k].at[i], p2[k].at[i])
+            delta = stat[k][u, 5:6] * stat[k][u, 4:5] + stat[k][u, 2:3] * stat[k][u, 3:4]
+            delta = delta + weighted(slice(0, HALF), e2[k].at[i], p2[k].at[i])
             stat[k][u, 6:7] = delta
             for c in range(HALF // CHUNK):
                 rows = slice(c * CHUNK, (c + 1) * CHUNK)
@@ -281,9 +298,9 @@
             k, u, q, g = unit(pair, j)
             dqt[k][u] = matmul(kt_far[...], ds_far[k][:, j // 2 * PAIR : (j // 2 + 1) * PAIR])
 
-    def near_rows(pair, j, low, high):
+    def near_rows(pair, j, low, high, line):
         k, u = j % 2, 2 * pair + j // 2
-        a1, delta = stat[k][u, 5:6], stat[k][u, 6:7]
+        a1, delta = stat[k][u, line : line + 1], stat[k][u, 6:7]
         for c in range(low // CHUNK, high // CHUNK):
             rows = slice(c * CHUNK, (c + 1) * CHUNK)
             p = e1[k][u, rows] * a1
@@ -298,13 +315,13 @@
 
     def old_work(pair):
         for j in range(HEADS):
-            near_rows(pair, j, 0, HALF - j * BLOCK)
+            near_rows(pair, j, 0, HALF - j * BLOCK, 2)
         for j in range(HEADS):
             near_keys(pair, j, 0, HALF - j * BLOCK)
 
     def own_work(pair):
         for j in range(HEADS):
-            near_rows(pair, j, HALF - j * BLOCK, NEAR)
+            near_rows(pair, j, HALF - j * BLOCK, NEAR, 5)
         for j in range(HEADS):
             near_keys(pair, j, HALF - j * BLOCK, NEAR)
             k, u = j % 2, 2 * pair + j // 2
@@ -339,26 +356,39 @@
 
     for pair in range(2):
         unpack(pair, 0)
-        near_scores(pair)
+        own_scores(pair)
         if pair == 0:
             unpack(pair, 1)
-            near_values(pair)
+            own_values(pair)
+
+            @pl.when(has_old)
+            def _():
+                wait(old_in, old_sem)
+
+            kv[:, 0:HALF] = old_in[...]
+            kt[:, 0:HALF] = old_in[0].T
+
             wait(far_k, far_sem.at[0])
             kt_far[...] = far_k[...].T
             far_scores(pair)
             far_sum(pair, 1, pr_far)
+            old_values(pair)
             wait(far_v, far_sem.at[1])
         else:
             far_scores(pair)
+            old_work(0)
+            own_work(0)
             unpack(pair, 1)
+            send_queries(0)
             far_sum(pair, 1, pr_far)
-            near_values(pair)
+            own_values(pair)
+            old_values(pair)
         far_values(pair)
         if pair == 0:
             far_queries(pair)
-        far_sum(pair, 0, ds_far)
-
-    old_work(0)
+        if pair == 0:
+            far_sum(pair, 0, ds_far)
+
     old_work(1)
     relay_out[...] = acc1[:, 0:HALF].astype(jnp.bfloat16)
     backward = remote(relay_out, relay_in, send.at[47], relay_sem, place(-2, y))
@@ -367,8 +397,8 @@
     def _():
         backward.start()
 
-    own_work(0)
-    send_queries(0)
+    far_sum(1, 0, ds_far)
+
     far_queries(1)
     own_work(1)
     send_queries(1)

time: 51.6 us -> 51.4 us (level)
  the two profiles are of different devices: /device:TPU:7 before, /device:TPU:32 now
where the time goes in v5:
time: 51.4 us; the launch traced here: 51.3 us
  Pallas kernels  50.7 us (99%)
  between operations  0.64 us (1%)
    pallas_call x1, Pallas kernels, local(): pl.pallas_call(kernel, out_shape=(wide, shares), in_specs=[anywhere] * 4...  48.6 us
    pallas_call x1, Pallas kernels, local(): pl.pallas_call(finish, out_shape=(wide, narrow, narrow), in_specs=[near,...  2.12 us

profile of v5, /device:TPU:32, one launch (start us, length us, event | category | flops | bytes accessed | tf_op | source)
XLA Modules:
  0.0 51.3 jit_solution(2319880353047326457)
XLA Ops:
  0.6 48.6 %shard_map.76 = (bf16[128,2048]{1,0:T(8,128)(2,1)}, bf16[2,2,128,512]{3,2,1,0:T(8,128)(2,1)}) custom-call(bf16[128,2048]{1,0:T(8,128)(2,1)} %q_ref.1, bf16[128,512]{1,0:T(8,128)(2,1)} %k_ref.1, bf16[128,512]{1,0:T(8,128)(2,1)} %v_ref.1, bf16[128,2048]{1,0:T(8,128)(2,1)} %g_ref.1, s32[48]{0:T(128)} %len_ref.1), custom_call_target="tpu_custom_call" | custom-call | flops 3221225472 | bytes 3145728 | tf_op jit(solution)/shard_map/pallas_call | solution.py:446
  49.2 2.1 %shard_map.77 = (bf16[128,2048]{1,0:T(8,128)(2,1)}, bf16[128,512]{1,0:T(8,128)(2,1)}, bf16[128,512]{1,0:T(8,128)(2,1)}) custom-call(bf16[128,2048]{1,0:T(8,128)(2,1)} %get-tuple-element.5.dq_in, bf16[2,2,128,512]{3,2,1,0:T(8,128)(2,1)} %get-tuple-element.6.back), custom_call_target="tpu_custom_call" | custom-call | tf_op jit(solution)/shard_map/pallas_call | solution.py:512
